TPU v7x, 256 devices: a whole 4x4x8 slice. The times are simulated.
256 devices in a mesh: dp: 16 (over x, z_hi), context: 16 (over z_lo, y, core).
Axes of the slice: x: 4, y: 4, z: 8 (z_hi: 4, z_lo: 2; z = z_hi * 2 + z_lo), core: 2. Of those that a mesh axis runs over, the one named last changes fastest.
Arguments:
- query_act: bfloat16 [32768, 4096], P(('dp', 'context')), may hold values from -6 to 6
- key_act: bfloat16 [32768, 4096], P(('dp', 'context')), may hold values from -6 to 6
- value_act: bfloat16 [32768, 4096], P(('dp', 'context')), may hold values from -6 to 6
- out_grad: bfloat16 [32768, 4096], P(('dp', 'context')), may hold values from -24 to 24
- out_weight: bfloat16 [4096, 4096], P('context', 'dp'), may hold values from -0.09375 to 0.09375
- filter_taps: bfloat16 [2048, 4096], P('dp', 'context'), may hold values from -0.125 to 0.125
Outputs:
- query_grad: bfloat16 [32768, 4096], P(('dp', 'context'))
- key_grad: bfloat16 [32768, 4096], P(('dp', 'context'))
- value_grad: bfloat16 [32768, 4096], P(('dp', 'context'))
- weight_grad: float32 [4096, 4096], P('context', 'dp')
- filter_grad: float32 [2048, 4096], P('dp', 'context')
All inputs are finite; a program needn't handle non-finite values.
Results may differ from a plain program's by a relative error of at most 0.012.
Values may be sent and summed in bfloat16 or wider, within the bound.
A program may use at most 128 MiB of HBM per device.

v0:
```python
import math

import jax
import jax.numpy as jnp
from jax import lax
from jax.sharding import PartitionSpec as P

precise = lax.Precision.HIGHEST


def phase_grid(row_count, col_count, period):
    row_index = lax.broadcasted_iota(jnp.int32, (row_count, col_count), 0)
    col_index = lax.broadcasted_iota(jnp.int32, (row_count, col_count), 1)
    return (row_index * col_index % period).astype(jnp.float32) * (2.0 * math.pi / period)


def mixing_table(inner, sign):
    angle = phase_grid(inner, inner, inner)
    cosine = jnp.cos(angle)
    sine = jnp.sin(angle)
    return jnp.stack([jnp.stack([cosine, sign * sine]), jnp.stack([-sign * sine, cosine])])


def forward_half(signal, outer, inner):
    half = outer // 2
    width = half + 1
    channels = signal.shape[1]
    flat = signal.reshape(half, inner * channels)
    angle_one = phase_grid(width, half, outer)
    table_one = jnp.concatenate([jnp.cos(angle_one), -jnp.sin(angle_one)], axis=0)
    section = jnp.dot(table_one, flat, precision=precise).reshape(2, width, inner, channels)
    twist = phase_grid(width, inner, outer * inner)[:, :, None]
    twist_cos = jnp.cos(twist)
    twist_sin = jnp.sin(twist)
    turned = jnp.stack(
        [
            section[0] * twist_cos + section[1] * twist_sin,
            section[1] * twist_cos - section[0] * twist_sin,
        ]
    )
    return jnp.einsum("srxy,rkyc->skxc", mixing_table(inner, 1.0), turned, precision=precise)


def inverse_half(spectrum, outer, inner):
    half = outer // 2
    width = half + 1
    channels = spectrum.shape[3]
    mixed = jnp.einsum("srxy,rkyc->skxc", mixing_table(inner, -1.0), spectrum, precision=precise)
    twist = phase_grid(width, inner, outer * inner)[:, :, None]
    twist_cos = jnp.cos(twist)
    twist_sin = jnp.sin(twist)
    turned = jnp.stack(
        [mixed[0] * twist_cos - mixed[1] * twist_sin, mixed[0] * twist_sin + mixed[1] * twist_cos]
    )
    turned = turned.reshape(2 * width, inner * channels)
    angle_two = phase_grid(half, width, outer)
    freq_index = lax.broadcasted_iota(jnp.int32, (half, width), 1)
    weights = jnp.where((freq_index == 0) | (freq_index == half), 1.0, 2.0).astype(jnp.float32)
    table_two = jnp.concatenate(
        [weights * jnp.cos(angle_two), -weights * jnp.sin(angle_two)], axis=1
    )
    result = jnp.dot(table_two, turned, precision=precise) / (outer * inner)
    return result.reshape(half * inner, channels)


def spectral_product(left, right, conjugate):
    left_re = left[0]
    left_im = -left[1] if conjugate else left[1]
    right_re = right[0]
    right_im = right[1]
    return jnp.stack(
        [left_re * right_re - left_im * right_im, left_re * right_im + left_im * right_re]
    )


def shards(query_act, key_act, value_act, out_grad, out_weight, filter_taps):
    tok_rows = query_act.shape[0]
    ctx_count = lax.axis_size("context")
    dp_count = lax.axis_size("dp")
    outer = 2 * tok_rows
    query_chan, key_chan, value_chan = (
        lax.all_to_all(query_act, "context", split_axis=1, concat_axis=0, tiled=True),
        lax.all_to_all(key_act, "context", split_axis=1, concat_axis=0, tiled=True),
        lax.all_to_all(value_act, "context", split_axis=1, concat_axis=0, tiled=True),
    )
    prod_chan = (key_chan.astype(jnp.float32) * value_chan.astype(jnp.float32)).astype(jnp.bfloat16)
    weight_block = lax.all_gather(out_weight, "dp", axis=1, tiled=True)
    taps_block = lax.all_gather(filter_taps, "dp", axis=0, tiled=True)
    spec_filter = forward_half(taps_block.astype(jnp.float32), outer, ctx_count)
    spec_prod = forward_half(prod_chan.astype(jnp.float32), outer, ctx_count)
    conv_out = inverse_half(spectral_product(spec_filter, spec_prod, False), outer, ctx_count)
    query_f32 = query_chan.astype(jnp.float32)
    gated = (query_f32 * conv_out).astype(jnp.bfloat16)
    cotangent = lax.all_gather(out_grad, "context", axis=0, tiled=True)
    grad_gated = jnp.einsum(
        "tj,ij->ti", cotangent, weight_block, preferred_element_type=jnp.float32
    )
    weight_term = jnp.einsum("ti,tj->ij", gated, cotangent, preferred_element_type=jnp.float32)
    grad_query = (grad_gated * conv_out).astype(jnp.bfloat16)
    grad_conv = grad_gated * query_f32
    spec_grad = forward_half(grad_conv, outer, ctx_count)
    grad_prod = inverse_half(
        spectral_product(spec_filter, spec_grad, True), outer, ctx_count
    ).astype(jnp.bfloat16)
    filter_term = inverse_half(spectral_product(spec_prod, spec_grad, True), outer, ctx_count)
    weight_grad = lax.psum_scatter(weight_term, "dp", scatter_dimension=1, tiled=True) / dp_count
    filter_grad = lax.psum_scatter(filter_term, "dp", scatter_dimension=0, tiled=True) / dp_count
    grad_key_chan = (grad_prod.astype(jnp.float32) * value_chan.astype(jnp.float32)).astype(
        jnp.bfloat16
    )
    grad_value_chan = (grad_prod.astype(jnp.float32) * key_chan.astype(jnp.float32)).astype(
        jnp.bfloat16
    )
    query_grad, key_grad, value_grad = (
        lax.all_to_all(grad_query, "context", split_axis=0, concat_axis=1, tiled=True),
        lax.all_to_all(grad_key_chan, "context", split_axis=0, concat_axis=1, tiled=True),
        lax.all_to_all(grad_value_chan, "context", split_axis=0, concat_axis=1, tiled=True),
    )
    return (query_grad, key_grad, value_grad, weight_grad, filter_grad)


def solution(mesh):
    return jax.shard_map(
        shards,
        mesh=mesh,
        in_specs=(
            P(("dp", "context"), None),
            P(("dp", "context"), None),
            P(("dp", "context"), None),
            P(("dp", "context"), None),
            P("context", "dp"),
            P("dp", "context"),
        ),
        out_specs=(
            P(("dp", "context"), None),
            P(("dp", "context"), None),
            P(("dp", "context"), None),
            P("context", "dp"),
            P("dp", "context"),
        ),
        check_vma=False,
    )
```

profile of v0, /device:TPU:1, one launch (start us, length us, event | category | flops | bytes accessed | tf_op | source)
XLA Modules:
  0.0 504.0 jit_solution(13438743837616986989)
XLA Ops:
  7.2 0.7 all-gather.8.cloned.1.call-update
  7.9 0.7 all-gather.6.cloned.1.call-update
  8.7 0.7 all-gather.4.cloned.1.call-update
  9.4 2.4 copy.66
  11.8 7.3 %all-to-all-start = ((bf16[128,16,256]{2,0,1:T(8,128)(2,1)}), bf16[128,16,256]{2,0,1:T(8,128)(2,1)S(1)}, u32[]{:S(2)}, u32[]{:S(2)}) async-start(bf16[128,16,256]{2,0,1:T(8,128)(2,1)} %bitcast.230), calls=%async_computation | async-start | bytes 2097152 | tf_op jit(solution)/shard_map/all_to_all | solution.py:83
  19.1 1.1 copy.65
  20.2 15.5 %all-to-all-done = bf16[128,16,256]{2,0,1:T(8,128)(2,1)S(1)} async-done(((bf16[128,16,256]{2,0,1:T(8,128)(2,1)}), bf16[128,16,256]{2,0,1:T(8,128)(2,1)S(1)}, u32[]{:S(2)}, u32[]{:S(2)}) %all-to-all-start) | async-done | bytes 1048608 | tf_op jit(solution)/shard_map/all_to_all | solution.py:83
  35.7 4.3 all-to-all-start.1
  40.0 2.3 copy.64
  43.6 15.1 %all-to-all-done.1 = bf16[128,16,256]{2,0,1:T(8,128)(2,1)S(1)} async-done(((bf16[128,16,256]{2,0,1:T(8,128)(2,1)}), bf16[128,16,256]{2,0,1:T(8,128)(2,1)S(1)}, u32[]{:S(2)}, u32[]{:S(2)}) %all-to-all-start.1) | async-done | bytes 1048608 | tf_op jit(solution)/shard_map/all_to_all | solution.py:84
  58.7 5.0 all-to-all-start.3
  63.7 1.3 fusion.36
  65.0 2.3 convert_element_type.196
  67.3 3.1 fusion.44
  70.9 2.1 copy.54
  73.0 2.1 copy.55
  75.1 1.7 reshape.308
  76.9 1.8 fusion.45
  79.2 2.2 copy.52
  81.4 2.1 copy.53
  83.5 48.4 %all-gather.6.cloned.1.call-done = bf16[256,4096]{1,0:T(8,128)(2,1)} async-done(((bf16[256,256]{1,0:T(8,128)(2,1)}), bf16[256,4096]{1,0:T(8,128)(2,1)}) %all-gather.6.cloned.1.call-update) | async-done | bytes 2097168 | tf_op jit(solution)/shard_map/all_gather | solution.py:87
  131.9 94.2 %all-gather.4.cloned.1.call-done = bf16[2048,4096]{1,0:T(8,128)(2,1)} async-done(((bf16[128,4096]{1,0:T(8,128)(2,1)}), bf16[2048,4096]{1,0:T(8,128)(2,1)}) %all-gather.4.cloned.1.call-update) | async-done | bytes 16777232 | tf_op jit(solution)/shard_map/all_gather | solution.py:94
  226.1 13.4 %bitcast_multiply_fusion.9 = (f32[2048,256]{1,0:T(8,128)}, f32[2048,256]{1,0:T(8,128)}) fusion(bf16[128,16,256]{2,0,1:T(8,128)(2,1)} %all-to-all-done.3, bf16[2048,4096]{1,0:T(8,128)(2,1)} %all-gather.4.cloned.1.call-done, bf16[256,4096]{1,0:T(8,128)(2,1)} %all-gather.6.cloned.1.call-done), kind=kOutput, calls=%fused_computation.75 | convolution fusion | flops 4296015872 | bytes 24117248 | tf_op jit(solution)/shard_map/tj,ij->ti/dot_general | solution.py:95
  239.5 2.9 reshape.311
  242.4 5.1 %fusion.43 = f32[258,4096]{1,0:T(8,128)S(1)} fusion(f32[128,4096]{1,0:T(8,128)} %reshape.311, f32[129,128]{1,0:T(8,128)S(1)} %get-tuple-element.51, f32[129,128]{1,0:T(8,128)S(1)} %get-tuple-element.52), kind=kOutput, calls=%fused_computation.102 | convolution fusion | flops 1623228672 | bytes 6456320 | tf_op jit(solution)/shard_map/dot_general | solution.py:31
  248.1 0.7 copy.58
  248.9 0.7 copy.57
  249.7 0.7 copy-done.5
  250.4 0.9 copy-done.2
  251.3 0.6 copy-done.3
  251.9 3.3 fusion.26
  255.2 3.8 fusion.25
  259.1 3.8 fusion.22
  262.9 3.1 multiply_subtract_fusion.3
  266.0 4.0 fusion.24
  270.0 5.4 %multiply_subtract_fusion.1 = (f32[1,129,16,256]{3,2,0,1:T(8,128)}, f32[1,129,16,256]{3,2,0,1:T(8,128)}, f32[1,129,16,256]{3,2,0,1:T(8,128)}, f32[1,129,16,256]{3,2,0,1:T(8,128)}) fusion(f32[2,129,16,256]{3,2,0,1:T(8,128)S(1)} %fusion.22, f32[2,129,16,256]{3,2,0,1:T(8,128)S(1)} %fusion.24, f32[2,129,16,256]{3,2,0,1:T(8,128)S(1)} %fusion.25), kind=kLoop, calls=%fused_computation.58 | loop fusion | flops 6868992 | bytes 21135360 | tf_op jit(solution)/shard_map/sub | solution.py:72
  275.4 5.7 %fusion.21 = f32[2,129,16,256]{3,2,0,1:T(8,128)S(1)} fusion(f32[1,129,16,256]{3,2,0,1:T(8,128)} %get-tuple-element.8, f32[1,129,16,256]{3,2,0,1:T(8,128)} %get-tuple-element.7, f32[1,2,16,16]{3,2,1,0:T(8,128)S(1)} %get-tuple-element.48, f32[1,2,16,16]{3,2,1,0:T(8,128)S(1)} %get-tuple-element.43), kind=kOutput, calls=%fused_computation.36 | convolution fusion | flops 406856704 | bytes 8458240 | tf_op jit(solution)/shard_map/srxy,rkyc->skxc/dot_general | solution.py:48
  281.2 4.0 fusion.23
  285.2 4.0 fusion.20
  289.2 4.4 multiply_subtract_fusion
  295.1 3.9 copy.60
  299.0 5.2 %convolution_multiply_fusion = f32[128,4096]{1,0:T(8,128)} fusion(f32[258,4096]{1,0:T(8,128)S(1)} %bitcast.232, f32[128,129]{1,0:T(8,128)S(1)} %get-tuple-element.57, f32[128,129]{1,0:T(8,128)S(1)} %get-tuple-element.58), kind=kOutput, calls=%fused_computation | convolution fusion | flops 1623752960 | bytes 6456320 | tf_op jit(solution)/shard_map/dot_general | solution.py:62
  304.1 2.8 reshape.314
  307.4 2.8 pad_maximum_fusion
  311.2 3.9 copy.56
  315.1 5.1 %convolution_multiply_fusion.2 = f32[128,4096]{1,0:T(8,128)} fusion(f32[258,4096]{1,0:T(8,128)S(1)} %bitcast.233, f32[128,129]{1,0:T(8,128)S(1)} %get-tuple-element.57, f32[128,129]{1,0:T(8,128)S(1)} %get-tuple-element.58), kind=kOutput, calls=%fused_computation.2 | convolution fusion | flops 1623752960 | bytes 6456320 | tf_op jit(solution)/shard_map/dot_general | solution.py:62
  320.3 2.8 reshape.310
  323.1 3.9 fusion.35
  327.0 10.5 %fusion.89 = f32[256,4096]{1,0:T(8,128)} fusion(bf16[2048,256]{1,0:T(8,128)(2,1)S(1)} %get-tuple-element.31, bf16[2048,4096]{1,0:T(8,128)(2,1)} %all-gather.4.cloned.1.call-done), kind=kOutput, calls=%fused_computation.161 | convolution fusion | flops 4294967296 | bytes 22020096 | tf_op jit(solution)/shard_map/ti,tj->ij/dot_general | solution.py:98
  337.5 2.8 pad_maximum_fusion.1
  341.4 3.9 copy.59
  345.3 5.2 %fusion.1 = f32[128,4096]{1,0:T(8,128)} fusion(f32[258,4096]{1,0:T(8,128)S(1)} %bitcast.231, f32[128,129]{1,0:T(8,128)S(1)} %get-tuple-element.57, f32[128,129]{1,0:T(8,128)S(1)} %get-tuple-element.58), kind=kOutput, calls=%fused_computation.4 | convolution fusion | flops 1624801536 | bytes 6456320 | tf_op jit(solution)/shard_map/dot_general | solution.py:62
  350.5 2.9 reshape.316
  353.3 2.2 fusion.31
  355.6 21.8 %all_to_all.90 = bf16[16,128,256]{2,1,0:T(8,128)(2,1)S(1)} all-to-all(bf16[16,128,256]{2,1,0:T(8,128)(2,1)S(1)} %get-tuple-element.34), channel_id=1, replica_groups=mesh['dp'=16,'context'=16] {'context'}, dimensions={0} | all-to-all | bytes 2097152 | tf_op jit(solution)/shard_map/all_to_all | solution.py:116
  377.4 23.0 %all_to_all.91 = bf16[16,128,256]{2,1,0:T(8,128)(2,1)S(1)} all-to-all(bf16[16,128,256]{2,1,0:T(8,128)(2,1)S(1)} %get-tuple-element.33), channel_id=1, replica_groups=mesh['dp'=16,'context'=16] {'context'}, dimensions={0} | all-to-all | bytes 2097152 | tf_op jit(solution)/shard_map/all_to_all | solution.py:117
  400.4 3.9 all-to-all-start.2
  404.3 1.1 copy.50
  405.4 1.1 copy.51
  406.5 19.5 %all-to-all-done.2 = bf16[16,128,256]{2,1,0:T(8,128)(2,1)S(1)} async-done(((bf16[16,128,256]{2,1,0:T(8,128)(2,1)}), bf16[16,128,256]{2,1,0:T(8,128)(2,1)S(1)}, u32[]{:S(2)}, u32[]{:S(2)}) %all-to-all-start.2) | async-done | bytes 1048608 | tf_op jit(solution)/shard_map/all_to_all | solution.py:115
  426.0 1.1 copy.49
  427.1 1.6 broadcast_multiply_fusion.1
  428.7 66.9 %reduce-scatter.3.cloned.1.call-done = f32[256,256]{1,0:T(8,128)} async-done(((f32[256,4096]{1,0:T(8,128)}), f32[256,256]{1,0:T(8,128)}) %reduce-scatter.3.cloned.1.call-update) | async-done | bytes 262160 | tf_op jit(solution)/shard_map/reduce_scatter | solution.py:106
  495.6 1.7 broadcast_multiply_fusion
  (49 shorter events, 7.0 us)
Async XLA Ops:
  7.2 68.0 %all-gather.8.cloned.1.call-start = ((), (), s32[]{:S(2)}) async-start(), calls=%async_computation.10 | async-start | bytes 1114112 | tf_op jit(solution)/shard_map/all_gather | solution.py:88
  7.9 124.0 %all-gather.6.cloned.1.call-start = ((), (), s32[]{:S(2)}) async-start(), calls=%async_computation.9 | async-start | bytes 2228224 | tf_op jit(solution)/shard_map/all_gather | solution.py:87
  8.6 217.4 %all-gather.4.cloned.1.call-start = ((), (), s32[]{:S(2)}) async-start(), calls=%async_computation.8 | async-start | bytes 17825792 | tf_op jit(solution)/shard_map/all_gather | solution.py:94
  9.4 9.7 %copy-start.11 = (bf16[128,4096]{1,0:T(8,128)(2,1)S(1)}, bf16[128,4096]{1,0:T(8,128)(2,1)}, u32[]{:S(2)}) copy-start(bf16[128,4096]{1,0:T(8,128)(2,1)} %param.8) | copy-start | bytes 3145732
  11.8 23.9 %all-to-all-start = ((bf16[128,16,256]{2,0,1:T(8,128)(2,1)}), bf16[128,16,256]{2,0,1:T(8,128)(2,1)S(1)}, u32[]{:S(2)}, u32[]{:S(2)}) async-start(bf16[128,16,256]{2,0,1:T(8,128)(2,1)} %bitcast.230), calls=%async_computation | async-start | bytes 2097152 | tf_op jit(solution)/shard_map/all_to_all | solution.py:83
  35.7 23.0 %all-to-all-start.1 = ((bf16[128,16,256]{2,0,1:T(8,128)(2,1)}), bf16[128,16,256]{2,0,1:T(8,128)(2,1)S(1)}, u32[]{:S(2)}, u32[]{:S(2)}) async-start(bf16[128,16,256]{2,0,1:T(8,128)(2,1)} %bitcast.253), calls=%async_computation.1 | async-start | bytes 2097152 | tf_op jit(solution)/shard_map/all_to_all | solution.py:84
  58.7 6.3 %copy-start = (bf16[128,16,256]{2,0,1:T(8,128)(2,1)}, bf16[128,16,256]{2,0,1:T(8,128)(2,1)S(1)}, u32[]{:S(2)}) copy-start(bf16[128,16,256]{2,0,1:T(8,128)(2,1)S(1)} %all-to-all-done.1) | copy-start | bytes 3145732
  58.7 24.8 %all-to-all-start.3 = ((bf16[128,16,256]{2,0,1:T(8,128)(2,1)}), bf16[128,16,256]{2,0,1:T(8,128)(2,1)}, u32[]{:S(2)}, u32[]{:S(2)}) async-start(bf16[128,16,256]{2,0,1:T(8,128)(2,1)} %bitcast.252), calls=%async_computation.3 | async-start | bytes 2097152 | tf_op jit(solution)/shard_map/all_to_all | solution.py:82
  63.6 363.5 %reduce-scatter.5.cloned.1.call-start = ((), (), s32[]{:S(2)}) async-start(), calls=%async_computation.12 | async-start | bytes 2228224 | tf_op jit(solution)/shard_map/reduce_scatter | solution.py:107
  248.1 1.6 copy-start.4
  248.1 2.3 copy-start.5
  248.8 2.4 copy-start.2
  248.9 3.0 copy-start.3
  262.9 3.1 copy-start.10
  275.4 5.7 %copy-start.8 = (f32[1,129,16,256]{3,2,0,1:T(8,128)S(1)}, f32[1,129,16,256]{3,2,0,1:T(8,128)}, u32[]{:S(2)}) copy-start(f32[1,129,16,256]{3,2,0,1:T(8,128)} %get-tuple-element.29) | copy-start | bytes 6340612
  275.4 5.7 %copy-start.9 = (f32[1,129,16,256]{3,2,0,1:T(8,128)S(1)}, f32[1,129,16,256]{3,2,0,1:T(8,128)}, u32[]{:S(2)}) copy-start(f32[1,129,16,256]{3,2,0,1:T(8,128)} %get-tuple-element.30) | copy-start | bytes 6340612
  281.1 4.0 copy-start.6
  281.1 4.0 copy-start.7
  306.9 188.6 %reduce-scatter.3.cloned.1.call-start = ((), (), s32[]{:S(2)}) async-start(), calls=%async_computation.11 | async-start | bytes 4456448 | tf_op jit(solution)/shard_map/reduce_scatter | solution.py:106
  350.5 2.9 copy-start.1
  400.4 25.6 %all-to-all-start.2 = ((bf16[16,128,256]{2,1,0:T(8,128)(2,1)}), bf16[16,128,256]{2,1,0:T(8,128)(2,1)S(1)}, u32[]{:S(2)}, u32[]{:S(2)}) async-start(bf16[16,128,256]{2,1,0:T(8,128)(2,1)} %bitcast.29), calls=%async_computation.2 | async-start | bytes 2097152 | tf_op jit(solution)/shard_map/all_to_all | solution.py:115
Sparse Core Ops, SparseCore 0:
  10.4 58.7 all-gather.7
  71.6 60.2 all-gather.5
  133.7 92.3 all-gather.3
  307.1 89.0 reduce-scatter.4
  400.1 95.4 reduce-scatter.2
where the time goes:
time: 510 us; the launch traced here: 504 us
  waiting for transfers between devices  262 us (51%)
  matrix products  74.7 us (15%)
  local copies, waits for them, and re-layouts  53 us (10%)
  blocking collectives  44.9 us (9%)
  other arithmetic  34.2 us (7%)
  starting transfers between devices  21.1 us (4%)
  between operations  14.4 us (3%)
    all_gather x1, waiting for transfers between devices, shards(): cotangent = lax.all_gather(out_grad, 'context', axis=0, tiled=True)  94.2 us
    reduce_scatter x1, waiting for transfers between devices, shards(): lax.psum_scatter(weight_term, 'dp', scatter_dimension=1, tiled=True)  66.9 us
    all_gather x1, waiting for transfers between devices, shards(): weight_block = lax.all_gather(out_weight, 'dp', axis=1, tiled=True)  48.4 us
    unnamed x36, local copies, waits for them, and re-layouts  25.4 us
    all_to_all x1, blocking collectives, shards(): lax.all_to_all(grad_value_chan, 'context', split_axis=0, concat_axis=1, t...  23 us
    all_to_all x1, blocking collectives, shards(): lax.all_to_all(grad_key_chan, 'context', split_axis=0, concat_axis=1, til...  21.8 us
    all_to_all x1, waiting for transfers between devices, shards(): lax.all_to_all(grad_query, 'context', split_axis=0, concat_axis=1, tiled=...  19.5 us
    dot_general x3, matrix products, inverse_half(): result = jnp.dot(table_two, turned, precision=precise) / (outer * inner)  15.5 us
  transfers between devices with their start and end apart: 9, of which 6 were waited for; matrix products, arithmetic and copies ran while one was open for 16% of the time, Pallas kernels for 0%

commit v1 on v0

v1 whole, which is shorter than its diff:
```python
import math

import jax
import jax.numpy as jnp
import numpy as np
from jax import lax
from jax.experimental import pallas as pl
from jax.experimental.pallas import tpu as pltpu
from jax.sharding import PartitionSpec as P

SEQ = 2048
CHAN = 256
ROWS = 128
WIDTH = 4096
BLOCK = 512
PARTS = 4
SLAB = 1024
PIECE = 256
F32 = jnp.float32
BF16 = jnp.bfloat16
MESH = pl.DeviceIdType.MESH


def transform_tables():
    freq = np.concatenate([np.arange(0, BLOCK, 2), np.arange(1, BLOCK, 2)])
    time = np.arange(BLOCK)
    angle = ((2 * freq[:, None] + 1) * time[None, :] % (4 * BLOCK)) * (math.pi / (2 * BLOCK))
    table = np.concatenate([np.cos(angle), -np.sin(angle)], axis=0)
    return jnp.asarray(table, BF16), jnp.asarray(table.T / BLOCK, BF16)


def kernel(
    q_in, k_in, v_in, og_in, w_in, h_in, fwd_in, inv_in,
    qg_out, du_out, wg_out, fg_out,
    kv, ub, fwd, inv, cot, wrows, taps, qc, uc, spec_u, spec_g, spec_d, prod, zbuf, dgbuf, gtr, dzb, qgc, duc,
    wsend, wrecv, wown, wsend2, wrecv2, wfin, fsend, frecv, fown, fsend2, frecv2,
    lsem, ss_in, rs_in, ss_par, rs_par, ss_ag, rs_z, rs_ym, rs_yp, rs_zym, rs_zyp, rs_far, rs_sib,
    ss_w, rs_w, ss_w2, rs_w2, ss_f, rs_f, ss_out, rs_out,
):
    dp = lax.axis_index("dp")
    ctx = lax.axis_index("context")
    x, zh = dp // 4, dp % 4
    zl, y, core = ctx // 8, (ctx // 2) % 4, ctx % 2

    def ctx_dev(c):
        return {"dp": dp, "context": c}

    def dp_dev(xx, zz):
        return {"dp": xx * 4 + zz, "context": ctx}

    def ctx_of(zz, yy, kk):
        return zz * 8 + lax.rem(yy + 4, 4) * 2 + kk

    def remote(src, dst, send, recv, dev):
        return pltpu.make_async_remote_copy(
            src_ref=src, dst_ref=dst, send_sem=send, recv_sem=recv, device_id=dev, device_id_type=MESH
        )

    me = ctx_dev(lax.rem(ctx + 1, 16))

    def wait_recv(ref, send, recv):
        remote(ref, ref, send, recv, me).wait_recv()

    def wait_send(ref, send, recv):
        remote(ref, ref, send, recv, me).wait_send()

    def cols(i):
        return pl.ds(pl.multiple_of(i * PIECE, PIECE), PIECE)

    def rows(i, n):
        return pl.ds(pl.multiple_of(i * n, n), n)

    local_k = pltpu.make_async_copy(k_in, kv.at[0], lsem.at[0])
    local_v = pltpu.make_async_copy(v_in, kv.at[1], lsem.at[1])
    local_k.start()
    local_v.start()
    local_w = pltpu.make_async_copy(w_in, wrows.at[zh, :, cols(x)], lsem.at[5])
    local_h = pltpu.make_async_copy(h_in, taps.at[rows(dp, ROWS), :], lsem.at[6])
    local_h.start()
    local_w.start()
    local_q = pltpu.make_async_copy(q_in.at[:, cols(ctx)], qc.at[rows(ctx, ROWS), :], lsem.at[7])
    local_q.start()
    for part in range(PARTS):
        for xx in range(4):
            pltpu.make_async_copy(
                og_in.at[:, pl.ds((xx * 4 + part) * PIECE, PIECE)],
                cot.at[part, rows(ctx, ROWS), pl.ds(xx * PIECE, PIECE)],
                lsem.at[4],
            ).start()
    local_fwd = pltpu.make_async_copy(fwd_in, fwd, lsem.at[2])
    local_inv = pltpu.make_async_copy(inv_in, inv, lsem.at[3])
    local_fwd.start()
    local_inv.start()

    barrier = pltpu.get_barrier_semaphore()

    def greet(off, carry):
        pl.semaphore_signal(barrier, inc=1, device_id=ctx_dev(lax.rem(ctx + off, 16)), device_id_type=MESH)
        return carry

    lax.fori_loop(1, 16, greet, 0)
    for off in range(1, 4):
        pl.semaphore_signal(barrier, inc=1, device_id=dp_dev(lax.rem(x + off, 4), zh), device_id_type=MESH)
        pl.semaphore_signal(barrier, inc=1, device_id=dp_dev(x, lax.rem(zh + off, 4)), device_id_type=MESH)
    pl.semaphore_wait(barrier, 21)

    local_h.wait()
    local_w.wait()
    for off in range(1, 4):
        dev = dp_dev(x, lax.rem(zh + off, 4))
        own = taps.at[rows(dp, ROWS), :]
        remote(own, own, ss_par.at[0], rs_par.at[0], dev).start()

    def send_q(off, carry):
        c = lax.rem(ctx + off, 16)
        remote(q_in.at[:, cols(c)], qc.at[rows(ctx, ROWS), :], ss_in.at[0], rs_in.at[0], ctx_dev(c)).start()
        return carry

    lax.fori_loop(1, 16, send_q, 0)
    for off in range(1, 4):
        dev = dp_dev(x, lax.rem(zh + off, 4))
        own = wrows.at[zh, :, cols(x)]
        remote(own, own, ss_par.at[1], rs_par.at[1], dev).start()

    local_k.wait()
    local_v.wait()

    def product(i, carry):
        piece = cols(i)
        ub[:, piece] = (kv[0, :, piece].astype(F32) * kv[1, :, piece].astype(F32)).astype(BF16)
        return carry

    lax.fori_loop(0, 16, product, 0)
    local_u = pltpu.make_async_copy(ub.at[:, cols(ctx)], uc.at[rows(ctx, ROWS), :], lsem.at[8])
    local_u.start()

    def send_u(off, carry):
        c = lax.rem(ctx + off, 16)
        remote(ub.at[:, cols(c)], uc.at[rows(ctx, ROWS), :], ss_in.at[1], rs_in.at[1], ctx_dev(c)).start()
        return carry

    lax.fori_loop(1, 16, send_u, 0)

    dev_z = ctx_dev(ctx_of(1 - zl, y, core))
    dev_up = ctx_dev(ctx_of(zl, y + 1, core))
    dev_down = ctx_dev(ctx_of(zl, y - 1, core))
    dev_sib = ctx_dev(ctx_of(zl, y, 1 - core))

    def spread(part, c, start, count, recv, dev):
        piece = cot.at[part, pl.ds(pl.multiple_of(c * ROWS + start, 64), count), :]
        remote(piece, piece, ss_ag.at[part], recv.at[part], dev).start()

    def arrived(part, count, recv):
        wait_recv(cot.at[part, pl.ds(0, count), :], ss_ag.at[part], recv.at[part])

    def gather_own(part):
        spread(part, ctx, 0, ROWS, rs_z, dev_z)
        spread(part, ctx, 0, ROWS, rs_ym, dev_up)
        spread(part, ctx, 0, ROWS, rs_yp, dev_down)
        spread(part, ctx, 0, ROWS, rs_sib, dev_sib)

    def gather_pair(part):
        arrived(part, ROWS, rs_z)
        c = ctx_of(1 - zl, y, core)
        spread(part, c, 0, ROWS, rs_zym, dev_up)
        spread(part, c, 0, ROWS, rs_zyp, dev_down)
        spread(part, c, 0, ROWS, rs_sib, dev_sib)

    def gather_near(part, zz, from_down, from_up):
        arrived(part, ROWS, from_down)
        c = ctx_of(zz, y - 1, core)
        spread(part, c, 0, 64, rs_far, dev_up)
        spread(part, c, 0, ROWS, rs_sib, dev_sib)
        arrived(part, ROWS, from_up)
        c = ctx_of(zz, y + 1, core)
        spread(part, c, 64, 64, rs_far, dev_down)
        spread(part, c, 0, ROWS, rs_sib, dev_sib)

    def gather_far(part):
        arrived(part, 2 * ROWS, rs_far)
        spread(part, ctx_of(zl, y + 2, core), 0, ROWS, rs_sib, dev_sib)
        spread(part, ctx_of(1 - zl, y + 2, core), 0, ROWS, rs_sib, dev_sib)

    pltpu.make_async_copy(cot.at[0, pl.ds(0, 512), :], cot.at[0, pl.ds(0, 512), :], lsem.at[4]).wait()
    gather_own(0)
    gather_own(1)

    wait_recv(taps.at[pl.ds(0, 3 * ROWS), :], ss_par.at[0], rs_par.at[0])
    for off in range(1, 4):
        own = taps.at[rows(x, BLOCK), :]
        remote(own, own, ss_par.at[2], rs_par.at[2], dp_dev(lax.rem(x + off, 4), zh)).start()
    wait_recv(wrows.at[0, pl.ds(0, 192), :], ss_par.at[1], rs_par.at[1])
    for off in range(1, 4):
        own = wrows.at[:, :, cols(x)]
        remote(own, own, ss_par.at[3], rs_par.at[3], dp_dev(lax.rem(x + off, 4), zh)).start()

    def forward(source, spec):
        def step(i, carry):
            spec[i] = jnp.dot(fwd[...], source[rows(i, BLOCK), :], preferred_element_type=F32)
            return carry

        lax.fori_loop(0, 4, step, 0)

    def over_tiles(body):
        for half in range(2):
            sign = 1.0 - 2.0 * half

            def step(i, carry):
                base = pl.multiple_of(half * 256 + i * 16, 16)
                for lane in range(2):
                    body(pl.ds(base, 16), pl.ds(base + BLOCK, 16), pl.ds(lane * 128, 128), sign)
                return carry

            lax.fori_loop(0, 16, step, 0)

    local_fwd.wait()
    local_inv.wait()
    wait_recv(taps.at[pl.ds(0, 3 * BLOCK), :], ss_par.at[2], rs_par.at[2])
    forward(taps, spec_g)

    def window(re, im, lane, sign):
        for d in (3, 2, 1):
            real = spec_g[d, re, lane] - sign * spec_g[d - 1, im, lane]
            imag = spec_g[d, im, lane] + sign * spec_g[d - 1, re, lane]
            spec_g[d, re, lane] = real
            spec_g[d, im, lane] = imag

    over_tiles(window)

    local_u.wait()
    wait_recv(uc.at[pl.ds(0, 15 * ROWS), :], ss_in.at[1], rs_in.at[1])
    forward(uc, spec_u)
    gather_pair(0)

    def convolve(re, im, lane, sign):
        ure = [spec_u[a, re, lane] for a in range(4)]
        uim = [spec_u[a, im, lane] for a in range(4)]
        gre = [spec_g[a, re, lane] for a in range(4)]
        gim = [spec_g[a, im, lane] for a in range(4)]
        for i in range(4):
            prod[i, re, lane] = sum(ure[a] * gre[i - a] - uim[a] * gim[i - a] for a in range(i + 1)).astype(BF16)
            prod[i, im, lane] = sum(ure[a] * gim[i - a] + uim[a] * gre[i - a] for a in range(i + 1)).astype(BF16)

    over_tiles(convolve)
    local_q.wait()
    wait_recv(qc.at[pl.ds(0, 15 * ROWS), :], ss_in.at[0], rs_in.at[0])

    def conv_out(i, carry):
        out = jnp.dot(inv[...], prod[i], preferred_element_type=F32)
        zbuf[rows(i, BLOCK), :] = out
        return carry

    lax.fori_loop(0, 4, conv_out, 0)
    gather_near(0, zl, rs_ym, rs_yp)

    def gate(i, carry):
        block = rows(i, 256)
        gated = (qc[block, :].astype(F32) * zbuf[block, :]).astype(BF16).astype(F32)
        gtr[:, block] = gated.T.astype(BF16)
        dgbuf[block, :] = jnp.zeros((256, CHAN), F32)
        return carry

    lax.fori_loop(0, 8, gate, 0)
    wait_recv(wrows.at[pl.ds(0, 3)], ss_par.at[3], rs_par.at[3])

    def reduce_far(part):
        wait_recv(wrecv.at[part, pl.ds(0, 3)], ss_w.at[part], rs_w.at[part])
        total = wown[part]
        for off in range(1, 4):
            total = total + wrecv[part, lax.rem(x + off, 4)].astype(F32)

        @pl.when(zh == part)
        def _():
            wfin[...] = total

        @pl.when(zh != part)
        def _():
            wsend2[part] = total.astype(BF16)
            remote(wsend2.at[part], wrecv2.at[zh], ss_w2.at[0], rs_w2.at[0], dp_dev(x, part)).start()

    def slab(part, carry):
        gather_near(part, 1 - zl, rs_zym, rs_zyp)

        @pl.when(part < 3)
        def _():
            gather_pair(part + 1)

        @pl.when(part < 2)
        def _():
            gather_own(part + 2)

        gather_far(part)

        @pl.when(part < 3)
        def _():
            gather_near(part + 1, zl, rs_ym, rs_yp)

        arrived(part, 8 * ROWS, rs_sib)

        def grad_gated(i, carry):
            block = rows(i, BLOCK)
            dgbuf[block, :] += lax.dot_general(
                cot[part, block, :], wrows[part], (((1,), (1,)), ((), ())), preferred_element_type=F32
            )
            return carry

        def weight_term(i, carry):
            term = jnp.dot(gtr[...], cot[part, :, cols(i)], preferred_element_type=F32)
            wsend[part, i] = term.astype(BF16)

            @pl.when(i == x)
            def _():
                wown[part] = term

            return carry

        lax.fori_loop(0, 4, weight_term, 0)
        for off in range(1, 4):
            xx = lax.rem(x + off, 4)
            remote(wsend.at[part, xx], wrecv.at[part, x], ss_w.at[part], rs_w.at[part], dp_dev(xx, zh)).start()
        lax.fori_loop(0, 4, grad_gated, 0)

        @pl.when(part > 0)
        def _():
            reduce_far(part - 1)

        return carry

    lax.fori_loop(0, PARTS, slab, 0)

    def finish_dg(i, carry):
        block = rows(i, ROWS)
        grad = dgbuf[block, :]
        qgc[block, :] = (grad * zbuf[block, :]).astype(BF16)
        dzb[block, :] = (grad * qc[block, :].astype(F32)).astype(BF16)
        return carry

    lax.fori_loop(0, 16, finish_dg, 0)

    def send_back(source, target, index):
        own = pltpu.make_async_copy(source.at[rows(ctx, ROWS), :], target.at[:, cols(ctx)], lsem.at[9 + index])
        own.start()

        def step(off, carry):
            c = lax.rem(ctx + off, 16)
            remote(
                source.at[rows(c, ROWS), :], target.at[:, cols(ctx)], ss_out.at[index], rs_out.at[index], ctx_dev(c)
            ).start()
            return carry

        lax.fori_loop(1, 16, step, 0)
        return own

    own_qg = send_back(qgc, qg_out, 0)
    forward(dzb, spec_d)

    def correlate(re, im, lane, sign):
        gre = [spec_g[a, re, lane] for a in range(4)]
        gim = [spec_g[a, im, lane] for a in range(4)]
        dre = [spec_d[a, re, lane] for a in range(4)]
        dim = [spec_d[a, im, lane] for a in range(4)]
        for a in range(4):
            prod[a, re, lane] = sum(gre[i - a] * dre[i] + gim[i - a] * dim[i] for i in range(a, 4)).astype(BF16)
            prod[a, im, lane] = sum(gre[i - a] * dim[i] - gim[i - a] * dre[i] for i in range(a, 4)).astype(BF16)

    over_tiles(correlate)

    def grad_prod(i, carry):
        duc[rows(i, BLOCK), :] = jnp.dot(inv[...], prod[i], preferred_element_type=F32).astype(BF16)
        return carry

    lax.fori_loop(0, 4, grad_prod, 0)
    own_du = send_back(duc, du_out, 1)
    reduce_far(3)

    def filter_product(re, im, lane, sign):
        ure = [spec_u[a, re, lane] for a in range(4)]
        uim = [spec_u[a, im, lane] for a in range(4)]
        dre = [spec_d[a, re, lane] for a in range(4)]
        dim = [spec_d[a, im, lane] for a in range(4)]
        after = None
        for d in (3, 2, 1, 0):
            real = sum(ure[a] * dre[a + d] + uim[a] * dim[a + d] for a in range(4 - d))
            imag = sum(ure[a] * dim[a + d] - uim[a] * dre[a + d] for a in range(4 - d))
            if after is None:
                prod[d, re, lane] = real.astype(BF16)
                prod[d, im, lane] = imag.astype(BF16)
            else:
                prod[d, re, lane] = (real + sign * after[1]).astype(BF16)
                prod[d, im, lane] = (imag - sign * after[0]).astype(BF16)
            after = (real, imag)

    over_tiles(filter_product)

    def filter_term(i, carry):
        term = jnp.dot(inv[...], prod[i], preferred_element_type=F32)
        fsend[i] = term.astype(BF16)

        @pl.when(i == x)
        def _():
            fown[...] = term

        return carry

    lax.fori_loop(0, 4, filter_term, 0)
    for off in range(1, 4):
        xx = lax.rem(x + off, 4)
        remote(fsend.at[xx], frecv.at[x], ss_f.at[0], rs_f.at[0], dp_dev(xx, zh)).start()
    wait_recv(frecv.at[pl.ds(0, 3)], ss_f.at[0], rs_f.at[0])
    for off in range(1, 4):
        fown[...] += frecv[lax.rem(x + off, 4)].astype(F32)
    for off in range(1, 4):
        zz = lax.rem(zh + off, 4)
        fsend2[zz] = fown[rows(zz, ROWS), :].astype(BF16)
        remote(fsend2.at[zz], frecv2.at[zh], ss_f.at[1], rs_f.at[1], dp_dev(x, zz)).start()

    wait_recv(wrecv2.at[pl.ds(0, 3)], ss_w2.at[0], rs_w2.at[0])
    weight = wfin[...]
    for off in range(1, 4):
        weight = weight + wrecv2[lax.rem(zh + off, 4)].astype(F32)
    wg_out[...] = weight * (1.0 / 16.0)
    wait_recv(frecv2.at[pl.ds(0, 3)], ss_f.at[1], rs_f.at[1])
    grad = fown[rows(zh, ROWS), :]
    for off in range(1, 4):
        grad = grad + frecv2[lax.rem(zh + off, 4)].astype(F32)
    fg_out[...] = grad * (1.0 / 16.0)

    own_qg.wait()
    own_du.wait()
    for index in range(2):
        wait_send(uc.at[pl.ds(0, 15 * ROWS), :], ss_in.at[index], rs_in.at[index])
        wait_send(qgc.at[pl.ds(0, 15 * ROWS), :], ss_out.at[index], rs_out.at[index])
        wait_recv(qgc.at[pl.ds(0, 15 * ROWS), :], ss_out.at[index], rs_out.at[index])
    wait_send(taps.at[pl.ds(0, 3 * ROWS), :], ss_par.at[0], rs_par.at[0])
    wait_send(wrows.at[0, pl.ds(0, 192), :], ss_par.at[1], rs_par.at[1])
    wait_send(taps.at[pl.ds(0, 3 * BLOCK), :], ss_par.at[2], rs_par.at[2])
    wait_send(wrows.at[pl.ds(0, 3)], ss_par.at[3], rs_par.at[3])

    def drain(part, carry):
        wait_send(cot.at[part, pl.ds(0, 15 * ROWS), :], ss_ag.at[part], rs_z.at[part])
        wait_send(wsend.at[part, pl.ds(0, 3)], ss_w.at[part], rs_w.at[part])
        return carry

    lax.fori_loop(0, PARTS, drain, 0)
    wait_send(wsend2.at[pl.ds(0, 3)], ss_w2.at[0], rs_w2.at[0])
    wait_send(fsend.at[pl.ds(0, 3)], ss_f.at[0], rs_f.at[0])
    wait_send(fsend2.at[pl.ds(0, 3)], ss_f.at[1], rs_f.at[1])


def shards(query_act, key_act, value_act, out_grad, out_weight, filter_taps):
    fwd, inv = transform_tables()
    anywhere = pl.BlockSpec(memory_space=pl.ANY)
    inside = pl.BlockSpec(memory_space=pltpu.VMEM)
    dma = pltpu.SemaphoreType.DMA

    def vmem(shape, dtype):
        return pltpu.VMEM(shape, dtype)

    query_grad, grad_prod, weight_grad, filter_grad = pl.pallas_call(
        kernel,
        out_shape=(
            jax.ShapeDtypeStruct((ROWS, WIDTH), BF16),
            jax.ShapeDtypeStruct((ROWS, WIDTH), BF16),
            jax.ShapeDtypeStruct((CHAN, PIECE), F32),
            jax.ShapeDtypeStruct((ROWS, CHAN), F32),
        ),
        in_specs=[anywhere] * 8,
        out_specs=(anywhere, anywhere, inside, inside),
        scratch_shapes=[
            vmem((2, ROWS, WIDTH), BF16),
            vmem((ROWS, WIDTH), BF16),
            vmem((2 * BLOCK, BLOCK), BF16),
            vmem((BLOCK, 2 * BLOCK), BF16),
            vmem((PARTS, SEQ, SLAB), BF16),
            vmem((PARTS, CHAN, SLAB), BF16),
            vmem((SEQ, CHAN), BF16),
            vmem((SEQ, CHAN), BF16),
            vmem((SEQ, CHAN), BF16),
            vmem((4, 2 * BLOCK, CHAN), F32),
            vmem((4, 2 * BLOCK, CHAN), F32),
            vmem((4, 2 * BLOCK, CHAN), F32),
            vmem((4, 2 * BLOCK, CHAN), BF16),
            vmem((SEQ, CHAN), F32),
            vmem((SEQ, CHAN), F32),
            vmem((CHAN, SEQ), BF16),
            vmem((SEQ, CHAN), BF16),
            vmem((SEQ, CHAN), BF16),
            vmem((SEQ, CHAN), BF16),
            vmem((PARTS, 4, CHAN, PIECE), BF16),
            vmem((PARTS, 4, CHAN, PIECE), BF16),
            vmem((PARTS, CHAN, PIECE), F32),
            vmem((PARTS, CHAN, PIECE), BF16),
            vmem((4, CHAN, PIECE), BF16),
            vmem((CHAN, PIECE), F32),
            vmem((4, BLOCK, CHAN), BF16),
            vmem((4, BLOCK, CHAN), BF16),
            vmem((BLOCK, CHAN), F32),
            vmem((4, ROWS, CHAN), BF16),
            vmem((4, ROWS, CHAN), BF16),
            dma((11,)),
            dma((2,)), dma((2,)),
            dma((4,)), dma((4,)),
            dma((PARTS,)),
            dma((PARTS,)), dma((PARTS,)), dma((PARTS,)), dma((PARTS,)), dma((PARTS,)), dma((PARTS,)), dma((PARTS,)),
            dma((PARTS,)), dma((PARTS,)),
            dma((1,)), dma((1,)),
            dma((2,)), dma((2,)),
            dma((2,)), dma((2,)),
        ],
        compiler_params=pltpu.CompilerParams(
            collective_id=0, has_side_effects=True, vmem_limit_bytes=60 * 1024 * 1024
        ),
        cost_estimate=pl.CostEstimate(flops=16_000_000_000, bytes_accessed=16_000_000, transcendentals=0),
        name="hyena_backward",
    )(query_act, key_act, value_act, out_grad, out_weight, filter_taps, fwd, inv)
    spread = grad_prod.astype(F32)
    key_grad = (spread * value_act.astype(F32)).astype(BF16)
    value_grad = (spread * key_act.astype(F32)).astype(BF16)
    return query_grad, key_grad, value_grad, weight_grad, filter_grad


def solution(mesh):
    return jax.shard_map(
        shards,
        mesh=mesh,
        in_specs=(
            P(("dp", "context"), None),
            P(("dp", "context"), None),
            P(("dp", "context"), None),
            P(("dp", "context"), None),
            P("context", "dp"),
            P("dp", "context"),
        ),
        out_specs=(
            P(("dp", "context"), None),
            P(("dp", "context"), None),
            P(("dp", "context"), None),
            P("context", "dp"),
            P("dp", "context"),
        ),
        check_vma=False,
    )
```

time: 510 us -> 174 us (0.34)
  the two profiles are of different devices: /device:TPU:1 before, /device:TPU:25 now
where the time goes in v1:
time: 174 us
  Pallas kernels  167 us (96%)
  other arithmetic  3.25 us (2%)
  local copies, waits for them, and re-layouts  2.46 us (1%)
    pallas_call x1, Pallas kernels, shards(): pl.pallas_call(kernel, out_shape=(jax.ShapeDtypeStruct((ROWS, WIDTH), BF1...  167 us

profile of v1, /device:TPU:25, one launch (start us, length us, event | category | flops | bytes accessed | tf_op | source)
XLA Modules:
  0.0 173.6 jit_solution(7030496851735557288)
XLA Ops:
  0.6 0.0 copy-start.1
  0.6 0.0 copy-start
  0.7 167.2 %hyena_backward.1 = (bf16[128,4096]{1,0:T(8,128)(2,1)}, bf16[128,4096]{1,0:T(8,128)(2,1)}, f32[256,256]{1,0:T(8,128)}, f32[128,256]{1,0:T(8,128)}) custom-call(bf16[128,4096]{1,0:T(8,128)(2,1)} %q_in.1, bf16[128,4096]{1,0:T(8,128)(2,1)} %k_in.1, bf16[128,4096]{1,0:T(8,128)(2,1)} %v_in.1, bf16[128,4096]{1,0:T(8,128)(2,1)} %og_in.1, bf16[256,256]{1,0:T(8,128)(2,1)} %w_in.1, ...), custom_call_target="tpu_custom_call" | custom-call | flops 16000000000 | bytes 16000000 | tf_op jit(solution)/shard_map/hyena_backward/pallas_call | solution.py:459
  167.9 0.0 copy-done.1
  167.9 0.0 copy-done
  167.9 0.0 copy-start.2
  167.9 3.3 %fusion.1 = (bf16[128,4096]{1,0:T(8,128)(2,1)}, bf16[128,4096]{1,0:T(8,128)(2,1)}) fusion(bf16[128,4096]{1,0:T(8,128)(2,1)} %get-tuple-element.10, bf16[128,4096]{1,0:T(8,128)(2,1)S(1)} %copy-done, bf16[128,4096]{1,0:T(8,128)(2,1)S(1)} %copy-done.1), kind=kLoop, calls=%fused_computation.3 | loop fusion | flops 3670016 | bytes 5242880 | tf_op jit(solution)/shard_map/convert_element_type | solution.py:518
  171.2 0.0 copy-done.2
  171.2 0.0 copy-start.3
  171.2 0.0 copy-start.4
  171.2 1.0 copy.16
  172.2 0.1 copy-done.3
  172.3 0.7 copy.17
  173.0 0.0 copy-done.4
  173.0 0.7 copy.18
Async XLA Ops:
  0.6 167.3 %copy-start.1 = (bf16[128,4096]{1,0:T(8,128)(2,1)S(1)}, bf16[128,4096]{1,0:T(8,128)(2,1)}, u32[]{:S(2)}) copy-start(bf16[128,4096]{1,0:T(8,128)(2,1)} %v_in.1) | copy-start | bytes 3145732
  0.6 167.3 %copy-start = (bf16[128,4096]{1,0:T(8,128)(2,1)S(1)}, bf16[128,4096]{1,0:T(8,128)(2,1)}, u32[]{:S(2)}) copy-start(bf16[128,4096]{1,0:T(8,128)(2,1)} %k_in.1) | copy-start | bytes 3145732
  167.9 3.3 %copy-start.2 = (bf16[128,4096]{1,0:T(8,128)(2,1)S(1)}, bf16[128,4096]{1,0:T(8,128)(2,1)}, u32[]{:S(2)}) copy-start(bf16[128,4096]{1,0:T(8,128)(2,1)} %get-tuple-element.20) | copy-start | bytes 3145732
  171.2 1.1 copy-start.3
  171.2 1.8 %copy-start.4 = (f32[128,256]{1,0:T(8,128)S(1)}, f32[128,256]{1,0:T(8,128)}, u32[]{:S(2)}) copy-start(f32[128,256]{1,0:T(8,128)} %get-tuple-element.24) | copy-start | bytes 393220

commit v2 on v1

--- a/solution.py
+++ b/solution.py
@@ -16,6 +16,7 @@
 PARTS = 4
 SLAB = 1024
 PIECE = 256
+FAR_BY_PAIR = (0, 1, 2, 3)
 F32 = jnp.float32
 BF16 = jnp.bfloat16
 MESH = pl.DeviceIdType.MESH
@@ -33,9 +34,9 @@
     q_in, k_in, v_in, og_in, w_in, h_in, fwd_in, inv_in,
     qg_out, du_out, wg_out, fg_out,
     kv, ub, fwd, inv, cot, wrows, taps, qc, uc, spec_u, spec_g, spec_d, prod, zbuf, dgbuf, gtr, dzb, qgc, duc,
-    wsend, wrecv, wown, wsend2, wrecv2, wfin, fsend, frecv, fown, fsend2, frecv2,
-    lsem, ss_in, rs_in, ss_par, rs_par, ss_ag, rs_z, rs_ym, rs_yp, rs_zym, rs_zyp, rs_far, rs_sib,
-    ss_w, rs_w, ss_w2, rs_w2, ss_f, rs_f, ss_out, rs_out,
+    wsend, wrecv, wown, wsend2, wrecv2, wrelay, fsend, frecv, fown, fsend2, frecv2, frelay,
+    lsem, ss_in, rs_in, ss_par, rs_par, ss_ag, rs_z, rs_ym, rs_yp, rs_zym, rs_zyp, rs_far, rs_sib, rs_zfar, rs_zsib,
+    ss_w, rs_w, ss_w2, rs_w2, rs_relay, ss_f, rs_f, ss_out, rs_out,
 ):
     dp = lax.axis_index("dp")
     ctx = lax.axis_index("context")
@@ -105,22 +106,23 @@
     pl.semaphore_wait(barrier, 21)
 
     local_h.wait()
+    z_up = dp_dev(x, lax.rem(zh + 1, 4))
+    z_down = dp_dev(x, lax.rem(zh + 3, 4))
+
+    def send_taps(zz, start, count, index, dev):
+        piece = taps.at[pl.ds(pl.multiple_of((x * 4 + zz) * ROWS + start, 64), count), :]
+        remote(piece, piece, ss_par.at[0], rs_par.at[index], dev).start()
+
+    def send_rows(zz, start, count, index, dev):
+        piece = wrows.at[zz, pl.ds(start, count), cols(x)]
+        remote(piece, piece, ss_par.at[1], rs_par.at[index], dev).start()
+
+    send_taps(zh, 0, ROWS, 0, z_up)
+    send_taps(zh, 0, ROWS, 1, z_down)
+
     local_w.wait()
-    for off in range(1, 4):
-        dev = dp_dev(x, lax.rem(zh + off, 4))
-        own = taps.at[rows(dp, ROWS), :]
-        remote(own, own, ss_par.at[0], rs_par.at[0], dev).start()
-
-    def send_q(off, carry):
-        c = lax.rem(ctx + off, 16)
-        remote(q_in.at[:, cols(c)], qc.at[rows(ctx, ROWS), :], ss_in.at[0], rs_in.at[0], ctx_dev(c)).start()
-        return carry
-
-    lax.fori_loop(1, 16, send_q, 0)
-    for off in range(1, 4):
-        dev = dp_dev(x, lax.rem(zh + off, 4))
-        own = wrows.at[zh, :, cols(x)]
-        remote(own, own, ss_par.at[1], rs_par.at[1], dev).start()
+    send_rows(zh, 0, CHAN, 3, z_up)
+    send_rows(zh, 0, CHAN, 4, z_down)
 
     local_k.wait()
     local_v.wait()
@@ -133,13 +135,6 @@
     lax.fori_loop(0, 16, product, 0)
     local_u = pltpu.make_async_copy(ub.at[:, cols(ctx)], uc.at[rows(ctx, ROWS), :], lsem.at[8])
     local_u.start()
-
-    def send_u(off, carry):
-        c = lax.rem(ctx + off, 16)
-        remote(ub.at[:, cols(c)], uc.at[rows(ctx, ROWS), :], ss_in.at[1], rs_in.at[1], ctx_dev(c)).start()
-        return carry
-
-    lax.fori_loop(1, 16, send_u, 0)
 
     dev_z = ctx_dev(ctx_of(1 - zl, y, core))
     dev_up = ctx_dev(ctx_of(zl, y + 1, core))
@@ -153,8 +148,10 @@
     def arrived(part, count, recv):
         wait_recv(cot.at[part, pl.ds(0, count), :], ss_ag.at[part], recv.at[part])
 
-    def gather_own(part):
+    def gather_own_z(part):
         spread(part, ctx, 0, ROWS, rs_z, dev_z)
+
+    def gather_own_y(part):
         spread(part, ctx, 0, ROWS, rs_ym, dev_up)
         spread(part, ctx, 0, ROWS, rs_yp, dev_down)
         spread(part, ctx, 0, ROWS, rs_sib, dev_sib)
@@ -164,42 +161,86 @@
         c = ctx_of(1 - zl, y, core)
         spread(part, c, 0, ROWS, rs_zym, dev_up)
         spread(part, c, 0, ROWS, rs_zyp, dev_down)
-        spread(part, c, 0, ROWS, rs_sib, dev_sib)
-
-    def gather_near(part, zz, from_down, from_up):
+        spread(part, c, 0, ROWS, rs_zsib, dev_sib)
+
+    def gather_near(part, own):
+        zz = zl if own else 1 - zl
+        from_down, from_up = (rs_ym, rs_yp) if own else (rs_zym, rs_zyp)
+        far, sib = (rs_far, rs_sib) if own else (rs_zfar, rs_zsib)
+        halves = own or part not in FAR_BY_PAIR
         arrived(part, ROWS, from_down)
         c = ctx_of(zz, y - 1, core)
-        spread(part, c, 0, 64, rs_far, dev_up)
-        spread(part, c, 0, ROWS, rs_sib, dev_sib)
+        if halves:
+            spread(part, c, 0, 64, far, dev_up)
+        spread(part, c, 0, ROWS, sib, dev_sib)
         arrived(part, ROWS, from_up)
         c = ctx_of(zz, y + 1, core)
-        spread(part, c, 64, 64, rs_far, dev_down)
-        spread(part, c, 0, ROWS, rs_sib, dev_sib)
-
-    def gather_far(part):
-        arrived(part, 2 * ROWS, rs_far)
-        spread(part, ctx_of(zl, y + 2, core), 0, ROWS, rs_sib, dev_sib)
-        spread(part, ctx_of(1 - zl, y + 2, core), 0, ROWS, rs_sib, dev_sib)
+        if halves:
+            spread(part, c, 64, 64, far, dev_down)
+        spread(part, c, 0, ROWS, sib, dev_sib)
+
+    def gather_far(part, own):
+        zz = zl if own else 1 - zl
+        far, sib = (rs_far, rs_sib) if own else (rs_zfar, rs_zsib)
+        arrived(part, ROWS, far)
+        c = ctx_of(zz, y + 2, core)
+        if own and part in FAR_BY_PAIR:
+            spread(part, c, 0, ROWS, rs_zfar, dev_z)
+        spread(part, c, 0, ROWS, sib, dev_sib)
+
+    def complete(part, own):
+        arrived(part, 4 * ROWS, rs_sib if own else rs_zsib)
 
     pltpu.make_async_copy(cot.at[0, pl.ds(0, 512), :], cot.at[0, pl.ds(0, 512), :], lsem.at[4]).wait()
-    gather_own(0)
-    gather_own(1)
-
-    wait_recv(taps.at[pl.ds(0, 3 * ROWS), :], ss_par.at[0], rs_par.at[0])
+    gather_own_y(0)
+    gather_own_y(1)
+    gather_own_y(2)
+    for start, recv, dev, away in ((0, 0, z_up, 3), (64, 1, z_down, 1)):
+        wait_recv(taps.at[pl.ds(0, ROWS), :], ss_par.at[0], rs_par.at[recv])
+        send_taps(lax.rem(zh + away, 4), start, 64, 2, dev)
+    for start, recv, dev, away in ((0, 3, z_up, 3), (128, 4, z_down, 1)):
+        wait_recv(wrows.at[0, pl.ds(0, 64), :], ss_par.at[1], rs_par.at[recv])
+        send_rows(lax.rem(zh + away, 4), start, 128, 5, dev)
+
+    def send_u(off, carry):
+        c = lax.rem(ctx + off, 16)
+        remote(ub.at[:, cols(c)], uc.at[rows(ctx, ROWS), :], ss_in.at[1], rs_in.at[1], ctx_dev(c)).start()
+        return carry
+
+    lax.fori_loop(1, 16, send_u, 0)
+
+    def send_q(off, carry):
+        c = lax.rem(ctx + off, 16)
+        remote(q_in.at[:, cols(c)], qc.at[rows(ctx, ROWS), :], ss_in.at[0], rs_in.at[0], ctx_dev(c)).start()
+        return carry
+
+    lax.fori_loop(1, 16, send_q, 0)
+
+    gather_own_z(0)
+    gather_own_z(1)
+    gather_own_z(2)
+    gather_own_z(3)
+    gather_near(0, True)
+
+    wait_recv(taps.at[pl.ds(0, ROWS), :], ss_par.at[0], rs_par.at[2])
     for off in range(1, 4):
         own = taps.at[rows(x, BLOCK), :]
-        remote(own, own, ss_par.at[2], rs_par.at[2], dp_dev(lax.rem(x + off, 4), zh)).start()
-    wait_recv(wrows.at[0, pl.ds(0, 192), :], ss_par.at[1], rs_par.at[1])
+        remote(own, own, ss_par.at[2], rs_par.at[6], dp_dev(lax.rem(x + off, 4), zh)).start()
+    wait_recv(wrows.at[0, pl.ds(0, 64), :], ss_par.at[1], rs_par.at[5])
     for off in range(1, 4):
         own = wrows.at[:, :, cols(x)]
-        remote(own, own, ss_par.at[3], rs_par.at[3], dp_dev(lax.rem(x + off, 4), zh)).start()
-
-    def forward(source, spec):
-        def step(i, carry):
+        remote(own, own, ss_par.at[3], rs_par.at[7], dp_dev(lax.rem(x + off, 4), zh)).start()
+    gather_own_y(3)
+    gather_near(1, True)
+    gather_near(2, True)
+
+    def forward(source, spec, first, count):
+        def step(j, carry):
+            i = first + j
             spec[i] = jnp.dot(fwd[...], source[rows(i, BLOCK), :], preferred_element_type=F32)
             return carry
 
-        lax.fori_loop(0, 4, step, 0)
+        lax.fori_loop(0, count, step, 0)
 
     def over_tiles(body):
         for half in range(2):
@@ -215,8 +256,8 @@
 
     local_fwd.wait()
     local_inv.wait()
-    wait_recv(taps.at[pl.ds(0, 3 * BLOCK), :], ss_par.at[2], rs_par.at[2])
-    forward(taps, spec_g)
+    wait_recv(taps.at[pl.ds(0, 3 * BLOCK), :], ss_par.at[2], rs_par.at[6])
+    forward(taps, spec_g, 0, 4)
 
     def window(re, im, lane, sign):
         for d in (3, 2, 1):
@@ -229,8 +270,7 @@
 
     local_u.wait()
     wait_recv(uc.at[pl.ds(0, 15 * ROWS), :], ss_in.at[1], rs_in.at[1])
-    forward(uc, spec_u)
-    gather_pair(0)
+    forward(uc, spec_u, 0, 4)
 
     def convolve(re, im, lane, sign):
         ure = [spec_u[a, re, lane] for a in range(4)]
@@ -251,7 +291,6 @@
         return carry
 
     lax.fori_loop(0, 4, conv_out, 0)
-    gather_near(0, zl, rs_ym, rs_yp)
 
     def gate(i, carry):
         block = rows(i, 256)
@@ -261,118 +300,120 @@
         return carry
 
     lax.fori_loop(0, 8, gate, 0)
-    wait_recv(wrows.at[pl.ds(0, 3)], ss_par.at[3], rs_par.at[3])
-
-    def reduce_far(part):
+    def reduce_near(part):
         wait_recv(wrecv.at[part, pl.ds(0, 3)], ss_w.at[part], rs_w.at[part])
         total = wown[part]
         for off in range(1, 4):
             total = total + wrecv[part, lax.rem(x + off, 4)].astype(F32)
-
-        @pl.when(zh == part)
-        def _():
-            wfin[...] = total
-
-        @pl.when(zh != part)
+        wown[part] = total
+
+        @pl.when(lax.rem(zh + 2, 4) == part)
         def _():
             wsend2[part] = total.astype(BF16)
-            remote(wsend2.at[part], wrecv2.at[zh], ss_w2.at[0], rs_w2.at[0], dp_dev(x, part)).start()
-
-    def slab(part, carry):
-        gather_near(part, 1 - zl, rs_zym, rs_zyp)
-
-        @pl.when(part < 3)
-        def _():
-            gather_pair(part + 1)
-
-        @pl.when(part < 2)
-        def _():
-            gather_own(part + 2)
-
-        gather_far(part)
-
-        @pl.when(part < 3)
-        def _():
-            gather_near(part + 1, zl, rs_ym, rs_yp)
-
-        arrived(part, 8 * ROWS, rs_sib)
-
-        def grad_gated(i, carry):
-            block = rows(i, BLOCK)
+            for start, dev in ((0, z_up), (128, z_down)):
+                half = pl.ds(start, 128)
+                remote(
+                    wsend2.at[part, half, :], wrelay.at[part, half, :], ss_w2.at[0], rs_relay.at[part], dev
+                ).start()
+
+    def reduce_far(part):
+        for away, start, dev in ((1, 0, z_up), (3, 128, z_down)):
+            half = pl.ds(start, 128)
+
+            @pl.when(lax.rem(zh + away, 4) == part)
+            def _():
+                wait_recv(wrelay.at[part, half, :], ss_w2.at[0], rs_relay.at[part])
+                wown[part, half, :] += wrelay[part, half, :].astype(F32)
+                wsend2[part] = wown[part].astype(BF16)
+                remote(wsend2.at[part], wrecv2.at[away // 2], ss_w2.at[0], rs_w2.at[0], dev).start()
+
+    def weight_term(part):
+        def product_of(xx):
+            return jnp.dot(gtr[...], cot[part, :, cols(xx)], preferred_element_type=F32)
+
+        def step(off, carry):
+            xx = lax.rem(x + off, 4)
+            wsend[part, xx] = product_of(xx).astype(BF16)
+            remote(wsend.at[part, xx], wrecv.at[part, x], ss_w.at[part], rs_w.at[part], dp_dev(xx, zh)).start()
+            return carry
+
+        lax.fori_loop(1, 4, step, 0)
+        wown[part] = product_of(x)
+
+    def grad_gated(part, own):
+        zz = zl if own else 1 - zl
+
+        def step(i, carry):
+            block = rows(zz * 2 + i, BLOCK)
             dgbuf[block, :] += lax.dot_general(
                 cot[part, block, :], wrows[part], (((1,), (1,)), ((), ())), preferred_element_type=F32
             )
             return carry
 
-        def weight_term(i, carry):
-            term = jnp.dot(gtr[...], cot[part, :, cols(i)], preferred_element_type=F32)
-            wsend[part, i] = term.astype(BF16)
-
-            @pl.when(i == x)
-            def _():
-                wown[part] = term
-
-            return carry
-
-        lax.fori_loop(0, 4, weight_term, 0)
-        for off in range(1, 4):
-            xx = lax.rem(x + off, 4)
-            remote(wsend.at[part, xx], wrecv.at[part, x], ss_w.at[part], rs_w.at[part], dp_dev(xx, zh)).start()
-        lax.fori_loop(0, 4, grad_gated, 0)
-
-        @pl.when(part > 0)
+        lax.fori_loop(0, 2, step, 0)
+
+    def send_back(source, target, index, c):
+        @pl.when(c != ctx)
         def _():
-            reduce_far(part - 1)
-
-        return carry
-
-    lax.fori_loop(0, PARTS, slab, 0)
-
-    def finish_dg(i, carry):
-        block = rows(i, ROWS)
-        grad = dgbuf[block, :]
-        qgc[block, :] = (grad * zbuf[block, :]).astype(BF16)
-        dzb[block, :] = (grad * qc[block, :].astype(F32)).astype(BF16)
-        return carry
-
-    lax.fori_loop(0, 16, finish_dg, 0)
-
-    def send_back(source, target, index):
-        own = pltpu.make_async_copy(source.at[rows(ctx, ROWS), :], target.at[:, cols(ctx)], lsem.at[9 + index])
-        own.start()
-
-        def step(off, carry):
-            c = lax.rem(ctx + off, 16)
             remote(
                 source.at[rows(c, ROWS), :], target.at[:, cols(ctx)], ss_out.at[index], rs_out.at[index], ctx_dev(c)
             ).start()
+
+    def keep_back(source, target, index):
+        return pltpu.make_async_copy(source.at[rows(ctx, ROWS), :], target.at[:, cols(ctx)], lsem.at[9 + index])
+
+    def finish_dg(own):
+        zz = zl if own else 1 - zl
+
+        def step(off, carry):
+            c = zz * 8 + lax.rem(ctx + off, 8)
+            block = rows(c, ROWS)
+            grad = dgbuf[block, :]
+            qgc[block, :] = (grad * zbuf[block, :]).astype(BF16)
+            dzb[block, :] = (grad * qc[block, :].astype(F32)).astype(BF16)
+            send_back(qgc, qg_out, 0, c)
             return carry
 
-        lax.fori_loop(1, 16, step, 0)
-        return own
-
-    own_qg = send_back(qgc, qg_out, 0)
-    forward(dzb, spec_d)
-
-    def correlate(re, im, lane, sign):
-        gre = [spec_g[a, re, lane] for a in range(4)]
-        gim = [spec_g[a, im, lane] for a in range(4)]
-        dre = [spec_d[a, re, lane] for a in range(4)]
-        dim = [spec_d[a, im, lane] for a in range(4)]
-        for a in range(4):
-            prod[a, re, lane] = sum(gre[i - a] * dre[i] + gim[i - a] * dim[i] for i in range(a, 4)).astype(BF16)
-            prod[a, im, lane] = sum(gre[i - a] * dim[i] - gim[i - a] * dre[i] for i in range(a, 4)).astype(BF16)
-
-    over_tiles(correlate)
-
-    def grad_prod(i, carry):
-        duc[rows(i, BLOCK), :] = jnp.dot(inv[...], prod[i], preferred_element_type=F32).astype(BF16)
-        return carry
-
-    lax.fori_loop(0, 4, grad_prod, 0)
-    own_du = send_back(duc, du_out, 1)
-    reduce_far(3)
-
+        lax.fori_loop(0, 8, step, 0)
+        forward(dzb, spec_d, zz * 2, 2)
+
+    gather_pair(0)
+    gather_near(3, True)
+    gather_far(0, True)
+    gather_pair(1)
+    gather_far(1, True)
+    gather_far(2, True)
+    gather_pair(2)
+    wait_recv(wrows.at[pl.ds(0, 3)], ss_par.at[3], rs_par.at[7])
+    complete(0, True)
+    grad_gated(0, True)
+    gather_pair(3)
+    complete(1, True)
+    grad_gated(1, True)
+    gather_far(3, True)
+    complete(2, True)
+    grad_gated(2, True)
+    complete(3, True)
+    grad_gated(3, True)
+    finish_dg(True)
+    own_qg = keep_back(qgc, qg_out, 0)
+    own_qg.start()
+    for part in range(PARTS):
+        gather_near(part, False)
+        gather_far(part, False)
+        if part > 0:
+            grad_gated(part - 1, False)
+        if part == 3:
+            reduce_near(1)
+            reduce_far(0)
+        complete(part, False)
+        if part < 3:
+            weight_term(part)
+        if part == 2:
+            reduce_near(0)
+    grad_gated(3, False)
+    finish_dg(False)
+    weight_term(3)
     def filter_product(re, im, lane, sign):
         ure = [spec_u[a, re, lane] for a in range(4)]
         uim = [spec_u[a, im, lane] for a in range(4)]
@@ -392,45 +433,95 @@
 
     over_tiles(filter_product)
 
-    def filter_term(i, carry):
-        term = jnp.dot(inv[...], prod[i], preferred_element_type=F32)
-        fsend[i] = term.astype(BF16)
-
-        @pl.when(i == x)
-        def _():
-            fown[...] = term
-
-        return carry
-
-    lax.fori_loop(0, 4, filter_term, 0)
-    for off in range(1, 4):
+    def filter_of(xx):
+        return jnp.dot(inv[...], prod[xx], preferred_element_type=F32)
+
+    def filter_term(off, carry):
         xx = lax.rem(x + off, 4)
-        remote(fsend.at[xx], frecv.at[x], ss_f.at[0], rs_f.at[0], dp_dev(xx, zh)).start()
-    wait_recv(frecv.at[pl.ds(0, 3)], ss_f.at[0], rs_f.at[0])
-    for off in range(1, 4):
-        fown[...] += frecv[lax.rem(x + off, 4)].astype(F32)
-    for off in range(1, 4):
-        zz = lax.rem(zh + off, 4)
+        fsend[xx] = filter_of(xx).astype(BF16)
+        for away in (2, 1, 3, 0):
+            zz = lax.rem(zh + away, 4)
+            remote(
+                fsend.at[xx, rows(zz, ROWS), :], frecv.at[x, rows(zz, ROWS), :], ss_f.at[0], rs_f.at[zz], dp_dev(xx, zh)
+            ).start()
+        return carry
+
+    lax.fori_loop(1, 4, filter_term, 0)
+    fown[...] = filter_of(x)
+
+    def correlate(re, im, lane, sign):
+        gre = [spec_g[a, re, lane] for a in range(4)]
+        gim = [spec_g[a, im, lane] for a in range(4)]
+        dre = [spec_d[a, re, lane] for a in range(4)]
+        dim = [spec_d[a, im, lane] for a in range(4)]
+        for a in range(4):
+            prod[a, re, lane] = sum(gre[i - a] * dre[i] + gim[i - a] * dim[i] for i in range(a, 4)).astype(BF16)
+            prod[a, im, lane] = sum(gre[i - a] * dim[i] - gim[i - a] * dre[i] for i in range(a, 4)).astype(BF16)
+
+    over_tiles(correlate)
+
+    def grad_prod(i, send):
+        duc[rows(i, BLOCK), :] = jnp.dot(inv[...], prod[i], preferred_element_type=F32).astype(BF16)
+        if send:
+            send_grad_prod(i)
+
+    def send_grad_prod(i):
+        for k in range(4):
+            send_back(duc, du_out, 1, i * 4 + k)
+
+    away = (1 - zl) * 2
+    grad_prod(away, True)
+    reduce_near(2)
+    grad_prod(away + 1, False)
+
+    def grad_prod_own(j, carry):
+        grad_prod(zl * 2 + j, True)
+        return carry
+
+    lax.fori_loop(0, 2, grad_prod_own, 0)
+    own_du = keep_back(duc, du_out, 1)
+    own_du.start()
+    reduce_far(1)
+    reduce_near(3)
+    def filter_sum(zz):
+        wait_recv(frecv.at[0, pl.ds(0, 3 * ROWS), :], ss_f.at[0], rs_f.at[zz])
+        total = fown[rows(zz, ROWS), :]
+        for off in range(1, 4):
+            total = total + frecv[lax.rem(x + off, 4), rows(zz, ROWS), :].astype(F32)
+        return total
+
+    opposite = lax.rem(zh + 2, 4)
+    fsend2[opposite] = filter_sum(opposite).astype(BF16)
+    for start, index, dev in ((0, 0, z_up), (64, 1, z_down)):
+        half = pl.ds(start, 64)
+        remote(fsend2.at[opposite, half, :], frelay.at[half, :], ss_f.at[1], rs_f.at[5 + index], dev).start()
+    send_grad_prod((1 - zl) * 2 + 1)
+    reduce_far(2)
+    for away, start, index, dev in ((1, 0, 0, z_up), (3, 64, 1, z_down)):
+        zz = lax.rem(zh + away, 4)
+        half = pl.ds(start, 64)
+        fown[rows(zz, ROWS), :] = filter_sum(zz)
+        wait_recv(frelay.at[half, :], ss_f.at[1], rs_f.at[5 + index])
+        fown[pl.ds(pl.multiple_of(zz * ROWS + start, 64), 64), :] += frelay[half, :].astype(F32)
         fsend2[zz] = fown[rows(zz, ROWS), :].astype(BF16)
-        remote(fsend2.at[zz], frecv2.at[zh], ss_f.at[1], rs_f.at[1], dp_dev(x, zz)).start()
-
-    wait_recv(wrecv2.at[pl.ds(0, 3)], ss_w2.at[0], rs_w2.at[0])
-    weight = wfin[...]
-    for off in range(1, 4):
-        weight = weight + wrecv2[lax.rem(zh + off, 4)].astype(F32)
-    wg_out[...] = weight * (1.0 / 16.0)
-    wait_recv(frecv2.at[pl.ds(0, 3)], ss_f.at[1], rs_f.at[1])
-    grad = fown[rows(zh, ROWS), :]
-    for off in range(1, 4):
-        grad = grad + frecv2[lax.rem(zh + off, 4)].astype(F32)
-    fg_out[...] = grad * (1.0 / 16.0)
-
+        remote(fsend2.at[zz], frecv2.at[index], ss_f.at[1], rs_f.at[4], dev).start()
+    grad = filter_sum(zh)
+
+    reduce_far(3)
     own_qg.wait()
     own_du.wait()
+    wait_recv(qgc.at[pl.ds(0, 15 * ROWS), :], ss_out.at[0], rs_out.at[0])
+    wait_recv(qgc.at[pl.ds(0, 15 * ROWS), :], ss_out.at[1], rs_out.at[1])
+    wait_recv(wrecv2, ss_w2.at[0], rs_w2.at[0])
+    weight = wown[zh] + wrecv2[0].astype(F32) + wrecv2[1].astype(F32)
+    wg_out[...] = weight * (1.0 / 16.0)
+    wait_recv(frecv2, ss_f.at[1], rs_f.at[4])
+    grad = grad + frecv2[0].astype(F32) + frecv2[1].astype(F32)
+    fg_out[...] = grad * (1.0 / 16.0)
+
     for index in range(2):
         wait_send(uc.at[pl.ds(0, 15 * ROWS), :], ss_in.at[index], rs_in.at[index])
         wait_send(qgc.at[pl.ds(0, 15 * ROWS), :], ss_out.at[index], rs_out.at[index])
-        wait_recv(qgc.at[pl.ds(0, 15 * ROWS), :], ss_out.at[index], rs_out.at[index])
     wait_send(taps.at[pl.ds(0, 3 * ROWS), :], ss_par.at[0], rs_par.at[0])
     wait_send(wrows.at[0, pl.ds(0, 192), :], ss_par.at[1], rs_par.at[1])
     wait_send(taps.at[pl.ds(0, 3 * BLOCK), :], ss_par.at[2], rs_par.at[2])
@@ -444,7 +535,7 @@
     lax.fori_loop(0, PARTS, drain, 0)
     wait_send(wsend2.at[pl.ds(0, 3)], ss_w2.at[0], rs_w2.at[0])
     wait_send(fsend.at[pl.ds(0, 3)], ss_f.at[0], rs_f.at[0])
-    wait_send(fsend2.at[pl.ds(0, 3)], ss_f.at[1], rs_f.at[1])
+    wait_send(fsend2.at[pl.ds(0, 3)], ss_f.at[1], rs_f.at[4])
 
 
 def shards(query_act, key_act, value_act, out_grad, out_weight, filter_taps):
@@ -490,21 +581,22 @@
             vmem((PARTS, 4, CHAN, PIECE), BF16),
             vmem((PARTS, CHAN, PIECE), F32),
             vmem((PARTS, CHAN, PIECE), BF16),
-            vmem((4, CHAN, PIECE), BF16),
-            vmem((CHAN, PIECE), F32),
+            vmem((2, CHAN, PIECE), BF16),
+            vmem((PARTS, CHAN, PIECE), BF16),
             vmem((4, BLOCK, CHAN), BF16),
             vmem((4, BLOCK, CHAN), BF16),
             vmem((BLOCK, CHAN), F32),
             vmem((4, ROWS, CHAN), BF16),
-            vmem((4, ROWS, CHAN), BF16),
+            vmem((2, ROWS, CHAN), BF16),
+            vmem((ROWS, CHAN), BF16),
             dma((11,)),
             dma((2,)), dma((2,)),
-            dma((4,)), dma((4,)),
+            dma((4,)), dma((8,)),
             dma((PARTS,)),
-            dma((PARTS,)), dma((PARTS,)), dma((PARTS,)), dma((PARTS,)), dma((PARTS,)), dma((PARTS,)), dma((PARTS,)),
+            *[dma((PARTS,)) for _ in range(9)],
             dma((PARTS,)), dma((PARTS,)),
-            dma((1,)), dma((1,)),
-            dma((2,)), dma((2,)),
+            dma((1,)), dma((1,)), dma((PARTS,)),
+            dma((2,)), dma((7,)),
             dma((2,)), dma((2,)),
         ],
         compiler_params=pltpu.CompilerParams(

time: 174 us -> 142 us (0.82)
  the two profiles are of different devices: /device:TPU:25 before, /device:TPU:1 now
where the time goes in v2:
time: 142 us; the launch traced here: 141 us
  Pallas kernels  134 us (94%)
  other arithmetic  3.25 us (2%)
  local copies, waits for them, and re-layouts  2.46 us (2%)
    pallas_call x1, Pallas kernels, shards(): pl.pallas_call(kernel, out_shape=(jax.ShapeDtypeStruct((ROWS, WIDTH), BF1...  134 us
    convert_element_type x1, other arithmetic, shards(): value_grad = (spread * key_act.astype(F32)).astype(BF16)  3.25 us

profile of v2, /device:TPU:1, one launch (start us, length us, event | category | flops | bytes accessed | tf_op | source)
XLA Modules:
  0.0 140.6 jit_solution(9726159773440982896)
XLA Ops:
  0.6 0.0 copy-start.1
  0.6 0.0 copy-start
  0.7 134.2 %hyena_backward.1 = (bf16[128,4096]{1,0:T(8,128)(2,1)}, bf16[128,4096]{1,0:T(8,128)(2,1)}, f32[256,256]{1,0:T(8,128)}, f32[128,256]{1,0:T(8,128)}) custom-call(bf16[128,4096]{1,0:T(8,128)(2,1)} %q_in.1, bf16[128,4096]{1,0:T(8,128)(2,1)} %k_in.1, bf16[128,4096]{1,0:T(8,128)(2,1)} %v_in.1, bf16[128,4096]{1,0:T(8,128)(2,1)} %og_in.1, bf16[256,256]{1,0:T(8,128)(2,1)} %w_in.1, ...), custom_call_target="tpu_custom_call" | custom-call | flops 16000000000 | bytes 16000000 | tf_op jit(solution)/shard_map/hyena_backward/pallas_call | solution.py:550
  134.8 0.0 copy-done.1
  134.9 0.0 copy-done
  134.9 0.0 copy-start.2
  134.9 3.3 %fusion.1 = (bf16[128,4096]{1,0:T(8,128)(2,1)}, bf16[128,4096]{1,0:T(8,128)(2,1)}) fusion(bf16[128,4096]{1,0:T(8,128)(2,1)} %get-tuple-element.10, bf16[128,4096]{1,0:T(8,128)(2,1)S(1)} %copy-done, bf16[128,4096]{1,0:T(8,128)(2,1)S(1)} %copy-done.1), kind=kLoop, calls=%fused_computation.3 | loop fusion | flops 3670016 | bytes 5242880 | tf_op jit(solution)/shard_map/convert_element_type | solution.py:610
  138.1 0.0 copy-done.2
  138.1 0.0 copy-start.3
  138.1 0.0 copy-start.4
  138.1 1.0 copy.16
  139.1 0.1 copy-done.3
  139.2 0.7 copy.17
  139.9 0.0 copy-done.4
  139.9 0.7 copy.18
Async XLA Ops:
  0.6 134.2 %copy-start.1 = (bf16[128,4096]{1,0:T(8,128)(2,1)S(1)}, bf16[128,4096]{1,0:T(8,128)(2,1)}, u32[]{:S(2)}) copy-start(bf16[128,4096]{1,0:T(8,128)(2,1)} %v_in.1) | copy-start | bytes 3145732
  0.6 134.2 %copy-start = (bf16[128,4096]{1,0:T(8,128)(2,1)S(1)}, bf16[128,4096]{1,0:T(8,128)(2,1)}, u32[]{:S(2)}) copy-start(bf16[128,4096]{1,0:T(8,128)(2,1)} %k_in.1) | copy-start | bytes 3145732
  134.9 3.3 %copy-start.2 = (bf16[128,4096]{1,0:T(8,128)(2,1)S(1)}, bf16[128,4096]{1,0:T(8,128)(2,1)}, u32[]{:S(2)}) copy-start(bf16[128,4096]{1,0:T(8,128)(2,1)} %get-tuple-element.20) | copy-start | bytes 3145732
  138.1 1.1 copy-start.3
  138.1 1.8 %copy-start.4 = (f32[128,256]{1,0:T(8,128)S(1)}, f32[128,256]{1,0:T(8,128)}, u32[]{:S(2)}) copy-start(f32[128,256]{1,0:T(8,128)} %get-tuple-element.24) | copy-start | bytes 393220

commit v3 on v2

--- a/solution.py
+++ b/solution.py
@@ -16,7 +16,7 @@
 PARTS = 4
 SLAB = 1024
 PIECE = 256
-FAR_BY_PAIR = (0, 1, 2, 3)
+FAR_BY_PAIR = (0, 1, 2)
 F32 = jnp.float32
 BF16 = jnp.bfloat16
 MESH = pl.DeviceIdType.MESH
@@ -32,11 +32,11 @@
 
 def kernel(
     q_in, k_in, v_in, og_in, w_in, h_in, fwd_in, inv_in,
-    qg_out, du_out, wg_out, fg_out,
-    kv, ub, fwd, inv, cot, wrows, taps, qc, uc, spec_u, spec_g, spec_d, prod, zbuf, dgbuf, gtr, dzb, qgc, duc,
-    wsend, wrecv, wown, wsend2, wrecv2, wrelay, fsend, frecv, fown, fsend2, frecv2, frelay,
+    qg_out, kg_out, vg_out, wg_out, fg_out,
+    kv, ub, fwd, inv, cot, wrows, taps, qc, uc, spec_u, spec_g, spec_d, prod, zbuf, dgbuf, gtr, dzb, qgc, duc, dul,
+    wsend, wrecv, wown, wsend2, wrecv2, fsend, frecv, fown, fsend2, frecv2,
     lsem, ss_in, rs_in, ss_par, rs_par, ss_ag, rs_z, rs_ym, rs_yp, rs_zym, rs_zyp, rs_far, rs_sib, rs_zfar, rs_zsib,
-    ss_w, rs_w, ss_w2, rs_w2, rs_relay, ss_f, rs_f, ss_out, rs_out,
+    ss_w, rs_w, ss_w2, rs_w2, ss_f, rs_f, ss_out, rs_out,
 ):
     dp = lax.axis_index("dp")
     ctx = lax.axis_index("context")
@@ -202,24 +202,24 @@
         wait_recv(wrows.at[0, pl.ds(0, 64), :], ss_par.at[1], rs_par.at[recv])
         send_rows(lax.rem(zh + away, 4), start, 128, 5, dev)
 
-    def send_u(off, carry):
-        c = lax.rem(ctx + off, 16)
-        remote(ub.at[:, cols(c)], uc.at[rows(ctx, ROWS), :], ss_in.at[1], rs_in.at[1], ctx_dev(c)).start()
-        return carry
-
-    lax.fori_loop(1, 16, send_u, 0)
-
-    def send_q(off, carry):
-        c = lax.rem(ctx + off, 16)
-        remote(q_in.at[:, cols(c)], qc.at[rows(ctx, ROWS), :], ss_in.at[0], rs_in.at[0], ctx_dev(c)).start()
-        return carry
-
-    lax.fori_loop(1, 16, send_q, 0)
+    def send_input(source, target, index):
+        def step(off, carry):
+            for zz in (1 - zl, zl):
+                c = zz * 8 + lax.rem(ctx + off, 8)
+
+                @pl.when(c != ctx)
+                def _():
+                    remote(
+                        source.at[:, cols(c)], target.at[rows(ctx, ROWS), :], ss_in.at[index], rs_in.at[index], ctx_dev(c)
+                    ).start()
+
+            return carry
+
+        lax.fori_loop(0, 8, step, 0)
 
     gather_own_z(0)
+    send_input(ub, uc, 1)
     gather_own_z(1)
-    gather_own_z(2)
-    gather_own_z(3)
     gather_near(0, True)
 
     wait_recv(taps.at[pl.ds(0, ROWS), :], ss_par.at[0], rs_par.at[2])
@@ -230,8 +230,9 @@
     for off in range(1, 4):
         own = wrows.at[:, :, cols(x)]
         remote(own, own, ss_par.at[3], rs_par.at[7], dp_dev(lax.rem(x + off, 4), zh)).start()
-    gather_own_y(3)
     gather_near(1, True)
+    gather_pair(0)
+    send_input(q_in, qc, 0)
     gather_near(2, True)
 
     def forward(source, spec, first, count):
@@ -282,15 +283,17 @@
             prod[i, im, lane] = sum(ure[a] * gim[i - a] + uim[a] * gre[i - a] for a in range(i + 1)).astype(BF16)
 
     over_tiles(convolve)
-    local_q.wait()
-    wait_recv(qc.at[pl.ds(0, 15 * ROWS), :], ss_in.at[0], rs_in.at[0])
-
     def conv_out(i, carry):
         out = jnp.dot(inv[...], prod[i], preferred_element_type=F32)
         zbuf[rows(i, BLOCK), :] = out
         return carry
 
+    gather_pair(1)
+    gather_own_z(2)
+    gather_own_z(3)
     lax.fori_loop(0, 4, conv_out, 0)
+    local_q.wait()
+    wait_recv(qc.at[pl.ds(0, 15 * ROWS), :], ss_in.at[0], rs_in.at[0])
 
     def gate(i, carry):
         block = rows(i, 256)
@@ -300,32 +303,18 @@
         return carry
 
     lax.fori_loop(0, 8, gate, 0)
-    def reduce_near(part):
+
+    def reduce_slab(part):
         wait_recv(wrecv.at[part, pl.ds(0, 3)], ss_w.at[part], rs_w.at[part])
         total = wown[part]
         for off in range(1, 4):
             total = total + wrecv[part, lax.rem(x + off, 4)].astype(F32)
         wown[part] = total
 
-        @pl.when(lax.rem(zh + 2, 4) == part)
+        @pl.when(zh != part)
         def _():
             wsend2[part] = total.astype(BF16)
-            for start, dev in ((0, z_up), (128, z_down)):
-                half = pl.ds(start, 128)
-                remote(
-                    wsend2.at[part, half, :], wrelay.at[part, half, :], ss_w2.at[0], rs_relay.at[part], dev
-                ).start()
-
-    def reduce_far(part):
-        for away, start, dev in ((1, 0, z_up), (3, 128, z_down)):
-            half = pl.ds(start, 128)
-
-            @pl.when(lax.rem(zh + away, 4) == part)
-            def _():
-                wait_recv(wrelay.at[part, half, :], ss_w2.at[0], rs_relay.at[part])
-                wown[part, half, :] += wrelay[part, half, :].astype(F32)
-                wsend2[part] = wown[part].astype(BF16)
-                remote(wsend2.at[part], wrecv2.at[away // 2], ss_w2.at[0], rs_w2.at[0], dev).start()
+            remote(wsend2.at[part], wrecv2.at[zh], ss_w2.at[0], rs_w2.at[0], dp_dev(x, part)).start()
 
     def weight_term(part):
         def product_of(xx):
@@ -377,43 +366,77 @@
         lax.fori_loop(0, 8, step, 0)
         forward(dzb, spec_d, zz * 2, 2)
 
-    gather_pair(0)
-    gather_near(3, True)
     gather_far(0, True)
-    gather_pair(1)
     gather_far(1, True)
+    gather_pair(2)
     gather_far(2, True)
-    gather_pair(2)
     wait_recv(wrows.at[pl.ds(0, 3)], ss_par.at[3], rs_par.at[7])
     complete(0, True)
     grad_gated(0, True)
     gather_pair(3)
     complete(1, True)
     grad_gated(1, True)
-    gather_far(3, True)
     complete(2, True)
     grad_gated(2, True)
+    gather_near(0, False)
+    gather_far(0, False)
+    gather_near(1, False)
+    gather_near(2, False)
+    complete(0, False)
+    weight_term(0)
+    grad_gated(0, False)
+    gather_near(3, False)
+    gather_own_y(3)
+    gather_far(1, False)
+    complete(1, False)
+    weight_term(1)
+    grad_gated(1, False)
+    gather_far(2, False)
+    gather_far(3, False)
+    complete(2, False)
+    grad_gated(2, False)
+    complete(3, False)
+    grad_gated(3, False)
+    gather_near(3, True)
+    finish_dg(False)
+    reduce_slab(0)
+    weight_term(2)
+    gather_far(3, True)
+    reduce_slab(1)
     complete(3, True)
     grad_gated(3, True)
     finish_dg(True)
     own_qg = keep_back(qgc, qg_out, 0)
     own_qg.start()
-    for part in range(PARTS):
-        gather_near(part, False)
-        gather_far(part, False)
-        if part > 0:
-            grad_gated(part - 1, False)
-        if part == 3:
-            reduce_near(1)
-            reduce_far(0)
-        complete(part, False)
-        if part < 3:
-            weight_term(part)
-        if part == 2:
-            reduce_near(0)
-    grad_gated(3, False)
-    finish_dg(False)
+    reduce_slab(2)
+    def correlate(re, im, lane, sign):
+        gre = [spec_g[a, re, lane] for a in range(4)]
+        gim = [spec_g[a, im, lane] for a in range(4)]
+        dre = [spec_d[a, re, lane] for a in range(4)]
+        dim = [spec_d[a, im, lane] for a in range(4)]
+        for a in range(4):
+            prod[a, re, lane] = sum(gre[i - a] * dre[i] + gim[i - a] * dim[i] for i in range(a, 4)).astype(BF16)
+            prod[a, im, lane] = sum(gre[i - a] * dim[i] - gim[i - a] * dre[i] for i in range(a, 4)).astype(BF16)
+
+    over_tiles(correlate)
+
+    def grad_prod(i, carry):
+        duc[rows(i, BLOCK), :] = jnp.dot(inv[...], prod[i], preferred_element_type=F32).astype(BF16)
+        return carry
+
+    lax.fori_loop(0, 4, grad_prod, 0)
+
+    def send_grad_prod(off, carry):
+        c = lax.rem(ctx + off, 8)
+        send_back(duc, dul, 1, (1 - zl) * 8 + c)
+        send_back(duc, dul, 1, zl * 8 + c)
+        return carry
+
+    lax.fori_loop(0, 8, send_grad_prod, 0)
+    own_du = keep_back(duc, dul, 1)
+    own_du.start()
     weight_term(3)
+
     def filter_product(re, im, lane, sign):
         ure = [spec_u[a, re, lane] for a in range(4)]
         uim = [spec_u[a, im, lane] for a in range(4)]
@@ -449,40 +472,7 @@
     lax.fori_loop(1, 4, filter_term, 0)
     fown[...] = filter_of(x)
 
-    def correlate(re, im, lane, sign):
-        gre = [spec_g[a, re, lane] for a in range(4)]
-        gim = [spec_g[a, im, lane] for a in range(4)]
-        dre = [spec_d[a, re, lane] for a in range(4)]
-        dim = [spec_d[a, im, lane] for a in range(4)]
-        for a in range(4):
-            prod[a, re, lane] = sum(gre[i - a] * dre[i] + gim[i - a] * dim[i] for i in range(a, 4)).astype(BF16)
-            prod[a, im, lane] = sum(gre[i - a] * dim[i] - gim[i - a] * dre[i] for i in range(a, 4)).astype(BF16)
-
-    over_tiles(correlate)
-
-    def grad_prod(i, send):
-        duc[rows(i, BLOCK), :] = jnp.dot(inv[...], prod[i], preferred_element_type=F32).astype(BF16)
-        if send:
-            send_grad_prod(i)
-
-    def send_grad_prod(i):
-        for k in range(4):
-            send_back(duc, du_out, 1, i * 4 + k)
-
-    away = (1 - zl) * 2
-    grad_prod(away, True)
-    reduce_near(2)
-    grad_prod(away + 1, False)
-
-    def grad_prod_own(j, carry):
-        grad_prod(zl * 2 + j, True)
-        return carry
-
-    lax.fori_loop(0, 2, grad_prod_own, 0)
-    own_du = keep_back(duc, du_out, 1)
-    own_du.start()
-    reduce_far(1)
-    reduce_near(3)
+    reduce_slab(3)
     def filter_sum(zz):
         wait_recv(frecv.at[0, pl.ds(0, 3 * ROWS), :], ss_f.at[0], rs_f.at[zz])
         total = fown[rows(zz, ROWS), :]
@@ -490,35 +480,41 @@
             total = total + frecv[lax.rem(x + off, 4), rows(zz, ROWS), :].astype(F32)
         return total
 
-    opposite = lax.rem(zh + 2, 4)
-    fsend2[opposite] = filter_sum(opposite).astype(BF16)
-    for start, index, dev in ((0, 0, z_up), (64, 1, z_down)):
-        half = pl.ds(start, 64)
-        remote(fsend2.at[opposite, half, :], frelay.at[half, :], ss_f.at[1], rs_f.at[5 + index], dev).start()
-    send_grad_prod((1 - zl) * 2 + 1)
-    reduce_far(2)
-    for away, start, index, dev in ((1, 0, 0, z_up), (3, 64, 1, z_down)):
+    for away in (2, 1, 3):
         zz = lax.rem(zh + away, 4)
-        half = pl.ds(start, 64)
-        fown[rows(zz, ROWS), :] = filter_sum(zz)
-        wait_recv(frelay.at[half, :], ss_f.at[1], rs_f.at[5 + index])
-        fown[pl.ds(pl.multiple_of(zz * ROWS + start, 64), 64), :] += frelay[half, :].astype(F32)
-        fsend2[zz] = fown[rows(zz, ROWS), :].astype(BF16)
-        remote(fsend2.at[zz], frecv2.at[index], ss_f.at[1], rs_f.at[4], dev).start()
+        fsend2[zz] = filter_sum(zz).astype(BF16)
+        remote(fsend2.at[zz], frecv2.at[zh], ss_f.at[1], rs_f.at[4], dp_dev(x, zz)).start()
     grad = filter_sum(zh)
 
-    reduce_far(3)
     own_qg.wait()
     own_du.wait()
     wait_recv(qgc.at[pl.ds(0, 15 * ROWS), :], ss_out.at[0], rs_out.at[0])
     wait_recv(qgc.at[pl.ds(0, 15 * ROWS), :], ss_out.at[1], rs_out.at[1])
-    wait_recv(wrecv2, ss_w2.at[0], rs_w2.at[0])
-    weight = wown[zh] + wrecv2[0].astype(F32) + wrecv2[1].astype(F32)
+    def branch_grads(i, carry):
+        piece = cols(i)
+        grad = dul[:, piece].astype(F32)
+        value = (grad * kv[0, :, piece].astype(F32)).astype(BF16)
+        kv[0, :, piece] = (grad * kv[1, :, piece].astype(F32)).astype(BF16)
+        kv[1, :, piece] = value
+        return carry
+
+    lax.fori_loop(0, 16, branch_grads, 0)
+    write_k = pltpu.make_async_copy(kv.at[0], kg_out, lsem.at[0])
+    write_v = pltpu.make_async_copy(kv.at[1], vg_out, lsem.at[1])
+    write_k.start()
+    write_v.start()
+    wait_recv(wrecv2.at[pl.ds(0, 3)], ss_w2.at[0], rs_w2.at[0])
+    weight = wown[zh]
+    for off in range(1, 4):
+        weight = weight + wrecv2[lax.rem(zh + off, 4)].astype(F32)
     wg_out[...] = weight * (1.0 / 16.0)
-    wait_recv(frecv2, ss_f.at[1], rs_f.at[4])
-    grad = grad + frecv2[0].astype(F32) + frecv2[1].astype(F32)
+    wait_recv(frecv2.at[pl.ds(0, 3)], ss_f.at[1], rs_f.at[4])
+    for off in range(1, 4):
+        grad = grad + frecv2[lax.rem(zh + off, 4)].astype(F32)
     fg_out[...] = grad * (1.0 / 16.0)
 
+    write_k.wait()
+    write_v.wait()
     for index in range(2):
         wait_send(uc.at[pl.ds(0, 15 * ROWS), :], ss_in.at[index], rs_in.at[index])
         wait_send(qgc.at[pl.ds(0, 15 * ROWS), :], ss_out.at[index], rs_out.at[index])
@@ -538,6 +534,26 @@
     wait_send(fsend2.at[pl.ds(0, 3)], ss_f.at[1], rs_f.at[4])
 
 
+def hand_over(*refs):
+    sources, targets, stage, (load_sem, store_sem) = refs[:5], refs[5:10], refs[10:15], refs[15:]
+    loads, stores = [], []
+    for i, source in enumerate(sources):
+        parts = 2 if source.shape[1] == WIDTH else 1
+        count = source.shape[0] // parts
+        for part in range(parts):
+            piece = pl.ds(part * count, count)
+            n = len(loads)
+            loads.append(pltpu.make_async_copy(source.at[piece], stage[i].at[piece], load_sem.at[n]))
+            stores.append(pltpu.make_async_copy(stage[i].at[piece], targets[i].at[piece], store_sem.at[n]))
+    for load in loads:
+        load.start()
+    for load, store in zip(loads, stores):
+        load.wait()
+        store.start()
+    for store in stores:
+        store.wait()
+
+
 def shards(query_act, key_act, value_act, out_grad, out_weight, filter_taps):
     fwd, inv = transform_tables()
     anywhere = pl.BlockSpec(memory_space=pl.ANY)
@@ -547,16 +563,18 @@
     def vmem(shape, dtype):
         return pltpu.VMEM(shape, dtype)
 
-    query_grad, grad_prod, weight_grad, filter_grad = pl.pallas_call(
+    outs = (
+        jax.ShapeDtypeStruct((ROWS, WIDTH), BF16),
+        jax.ShapeDtypeStruct((ROWS, WIDTH), BF16),
+        jax.ShapeDtypeStruct((ROWS, WIDTH), BF16),
+        jax.ShapeDtypeStruct((CHAN, PIECE), F32),
+        jax.ShapeDtypeStruct((ROWS, CHAN), F32),
+    )
+    grads = pl.pallas_call(
         kernel,
-        out_shape=(
-            jax.ShapeDtypeStruct((ROWS, WIDTH), BF16),
-            jax.ShapeDtypeStruct((ROWS, WIDTH), BF16),
-            jax.ShapeDtypeStruct((CHAN, PIECE), F32),
-            jax.ShapeDtypeStruct((ROWS, CHAN), F32),
-        ),
+        out_shape=outs,
         in_specs=[anywhere] * 8,
-        out_specs=(anywhere, anywhere, inside, inside),
+        out_specs=(anywhere, anywhere, anywhere, inside, inside),
         scratch_shapes=[
             vmem((2, ROWS, WIDTH), BF16),
             vmem((ROWS, WIDTH), BF16),
@@ -577,26 +595,25 @@
             vmem((SEQ, CHAN), BF16),
             vmem((SEQ, CHAN), BF16),
             vmem((SEQ, CHAN), BF16),
+            vmem((ROWS, WIDTH), BF16),
             vmem((PARTS, 4, CHAN, PIECE), BF16),
             vmem((PARTS, 4, CHAN, PIECE), BF16),
             vmem((PARTS, CHAN, PIECE), F32),
             vmem((PARTS, CHAN, PIECE), BF16),
-            vmem((2, CHAN, PIECE), BF16),
-            vmem((PARTS, CHAN, PIECE), BF16),
+            vmem((4, CHAN, PIECE), BF16),
             vmem((4, BLOCK, CHAN), BF16),
             vmem((4, BLOCK, CHAN), BF16),
             vmem((BLOCK, CHAN), F32),
             vmem((4, ROWS, CHAN), BF16),
-            vmem((2, ROWS, CHAN), BF16),
-            vmem((ROWS, CHAN), BF16),
+            vmem((4, ROWS, CHAN), BF16),
             dma((11,)),
             dma((2,)), dma((2,)),
             dma((4,)), dma((8,)),
             dma((PARTS,)),
             *[dma((PARTS,)) for _ in range(9)],
             dma((PARTS,)), dma((PARTS,)),
-            dma((1,)), dma((1,)), dma((PARTS,)),
-            dma((2,)), dma((7,)),
+            dma((1,)), dma((1,)),
+            dma((2,)), dma((5,)),
             dma((2,)), dma((2,)),
         ],
         compiler_params=pltpu.CompilerParams(
@@ -605,10 +622,16 @@
         cost_estimate=pl.CostEstimate(flops=16_000_000_000, bytes_accessed=16_000_000, transcendentals=0),
         name="hyena_backward",
     )(query_act, key_act, value_act, out_grad, out_weight, filter_taps, fwd, inv)
-    spread = grad_prod.astype(F32)
-    key_grad = (spread * value_act.astype(F32)).astype(BF16)
-    value_grad = (spread * key_act.astype(F32)).astype(BF16)
-    return query_grad, key_grad, value_grad, weight_grad, filter_grad
+    return pl.pallas_call(
+        hand_over,
+        out_shape=outs,
+        in_specs=[anywhere] * 5,
+        out_specs=(anywhere,) * 5,
+        scratch_shapes=[vmem(out.shape, out.dtype) for out in outs] + [dma((8,)), dma((8,))],
+        compiler_params=pltpu.CompilerParams(vmem_limit_bytes=60 * 1024 * 1024),
+        cost_estimate=pl.CostEstimate(flops=0, bytes_accessed=7_000_000, transcendentals=0),
+        name="hand_over",
+    )(*grads)
 
 
 def solution(mesh):

time: 142 us -> 140 us (0.986)
  Pallas kernels: 134 us -> 139 us
  other arithmetic: 3.25 us -> 0 us
  local copies, waits for them, and re-layouts: 2.46 us -> 0 us
    pallas_call x1 -> x2, Pallas kernels: 134 us -> 139 us  [the longest x1 136 us: shards(): pl.pallas_call(kernel, out_shape=outs, in_specs=[anywhere] * 8, out_specs...]
    convert_element_type x1 -> x0, other arithmetic: 3.25 us -> none  [shards(): value_grad = (spread * key_act.astype(F32)).astype(BF16)]
    unnamed x13 -> x0, local copies, waits for them, and re-layouts: 2.46 us -> none
where the time goes in v3:
time: 140 us
  Pallas kernels  139 us (99%)
    pallas_call x1, Pallas kernels, shards(): pl.pallas_call(kernel, out_shape=outs, in_specs=[anywhere] * 8, out_specs...  136 us
    pallas_call x1, Pallas kernels, shards(): pl.pallas_call(hand_over, out_shape=outs, in_specs=[anywhere] * 5, out_sp...  2.96 us

profile of v3, /device:TPU:1, one launch (start us, length us, event | category | flops | bytes accessed | tf_op | source)
XLA Modules:
  0.0 140.0 jit_solution(446373129742255794)
XLA Ops:
  0.6 136.4 %hyena_backward.1 = (bf16[128,4096]{1,0:T(8,128)(2,1)}, bf16[128,4096]{1,0:T(8,128)(2,1)}, bf16[128,4096]{1,0:T(8,128)(2,1)}, f32[256,256]{1,0:T(8,128)}, f32[128,256]{1,0:T(8,128)}) custom-call(bf16[128,4096]{1,0:T(8,128)(2,1)} %q_in.1, bf16[128,4096]{1,0:T(8,128)(2,1)} %k_in.1, bf16[128,4096]{1,0:T(8,128)(2,1)} %v_in.1, bf16[128,4096]{1,0:T(8,128)(2,1)} %og_in.1, ...), custom_call_target="tpu_custom_call" | custom-call | flops 16000000000 | bytes 16000000 | tf_op jit(solution)/shard_map/hyena_backward/pallas_call | solution.py:573
  137.0 3.0 %hand_over.1 = (bf16[128,4096]{1,0:T(8,128)(2,1)}, bf16[128,4096]{1,0:T(8,128)(2,1)}, bf16[128,4096]{1,0:T(8,128)(2,1)}, f32[256,256]{1,0:T(8,128)}, f32[128,256]{1,0:T(8,128)}) custom-call(bf16[128,4096]{1,0:T(8,128)(2,1)} %get-tuple-element.10.refs_0_, bf16[128,4096]{1,0:T(8,128)(2,1)} %get-tuple-element.11.refs_1_, ...), custom_call_target="tpu_custom_call" | custom-call | bytes 7000000 | tf_op jit(solution)/shard_map/hand_over/pallas_call | solution.py:625

commit v4 on v3

--- a/solution.py
+++ b/solution.py
@@ -16,6 +16,7 @@
 PARTS = 4
 SLAB = 1024
 PIECE = 256
+HALF = 128
 FAR_BY_PAIR = (0, 1, 2)
 F32 = jnp.float32
 BF16 = jnp.bfloat16
@@ -33,8 +34,8 @@
 def kernel(
     q_in, k_in, v_in, og_in, w_in, h_in, fwd_in, inv_in,
     qg_out, kg_out, vg_out, wg_out, fg_out,
-    kv, ub, fwd, inv, cot, wrows, taps, qc, uc, spec_u, spec_g, spec_d, prod, zbuf, dgbuf, gtr, dzb, qgc, duc, dul,
-    wsend, wrecv, wown, wsend2, wrecv2, fsend, frecv, fown, fsend2, frecv2,
+    kv, ub, fwd, inv, cot, wrows, taps, qc, uc, spec_u, spec_g, spec_d, prod, zbuf, dgbuf, gtr, qgc, duc, dul,
+    wsend, wrecv, wown, wsend2, wrecv2, wfin, fsend, frecv, fown, fsend2, frecv2,
     lsem, ss_in, rs_in, ss_par, rs_par, ss_ag, rs_z, rs_ym, rs_yp, rs_zym, rs_zyp, rs_far, rs_sib, rs_zfar, rs_zsib,
     ss_w, rs_w, ss_w2, rs_w2, ss_f, rs_f, ss_out, rs_out,
 ):
@@ -75,19 +76,29 @@
     local_v = pltpu.make_async_copy(v_in, kv.at[1], lsem.at[1])
     local_k.start()
     local_v.start()
-    local_w = pltpu.make_async_copy(w_in, wrows.at[zh, :, cols(x)], lsem.at[5])
+    def side_of(zz):
+        return pl.ds(pl.multiple_of(x * PIECE + zz // 2 * HALF, HALF), HALF)
+
+    local_w = [
+        pltpu.make_async_copy(
+            w_in.at[:, pl.ds(half * HALF, HALF)], wrows.at[lax.rem(zh, 2) * 2 + half, :, side_of(zh)], lsem.at[5]
+        )
+        for half in range(2)
+    ]
     local_h = pltpu.make_async_copy(h_in, taps.at[rows(dp, ROWS), :], lsem.at[6])
     local_h.start()
-    local_w.start()
+    for copy in local_w:
+        copy.start()
     local_q = pltpu.make_async_copy(q_in.at[:, cols(ctx)], qc.at[rows(ctx, ROWS), :], lsem.at[7])
     local_q.start()
     for part in range(PARTS):
         for xx in range(4):
-            pltpu.make_async_copy(
-                og_in.at[:, pl.ds((xx * 4 + part) * PIECE, PIECE)],
-                cot.at[part, rows(ctx, ROWS), pl.ds(xx * PIECE, PIECE)],
-                lsem.at[4],
-            ).start()
+            for side in range(2):
+                pltpu.make_async_copy(
+                    og_in.at[:, pl.ds((xx * 4 + part // 2 + 2 * side) * PIECE + part % 2 * HALF, HALF)],
+                    cot.at[part, rows(ctx, ROWS), pl.ds(xx * PIECE + side * HALF, HALF)],
+                    lsem.at[4],
+                ).start()
     local_fwd = pltpu.make_async_copy(fwd_in, fwd, lsem.at[2])
     local_inv = pltpu.make_async_copy(inv_in, inv, lsem.at[3])
     local_fwd.start()
@@ -114,13 +125,13 @@
         remote(piece, piece, ss_par.at[0], rs_par.at[index], dev).start()
 
     def send_rows(zz, start, count, index, dev):
-        piece = wrows.at[zz, pl.ds(start, count), cols(x)]
+        piece = wrows.at[pl.ds(lax.rem(zz, 2) * 2, 2), pl.ds(start, count), side_of(zz)]
         remote(piece, piece, ss_par.at[1], rs_par.at[index], dev).start()
 
     send_taps(zh, 0, ROWS, 0, z_up)
     send_taps(zh, 0, ROWS, 1, z_down)
 
-    local_w.wait()
+    pltpu.make_async_copy(w_in, w_in, lsem.at[5]).wait()
     send_rows(zh, 0, CHAN, 3, z_up)
     send_rows(zh, 0, CHAN, 4, z_down)
 
@@ -309,12 +320,21 @@
         total = wown[part]
         for off in range(1, 4):
             total = total + wrecv[part, lax.rem(x + off, 4)].astype(F32)
-        wown[part] = total
-
-        @pl.when(zh != part)
-        def _():
-            wsend2[part] = total.astype(BF16)
-            remote(wsend2.at[part], wrecv2.at[zh], ss_w2.at[0], rs_w2.at[0], dp_dev(x, part)).start()
+        wsend2[part] = total.astype(BF16)
+        target = pl.ds(part % 2 * HALF, HALF)
+        for side in range(2):
+            source = pl.ds(side * HALF, HALF)
+            zz = part // 2 + 2 * side
+
+            @pl.when(zh == zz)
+            def _():
+                wfin[:, target] = total[:, side * HALF : (side + 1) * HALF]
+
+            @pl.when(zh != zz)
+            def _():
+                remote(
+                    wsend2.at[part, :, source], wrecv2.at[zh, :, target], ss_w2.at[0], rs_w2.at[0], dp_dev(x, zz)
+                ).start()
 
     def weight_term(part):
         def product_of(xx):
@@ -359,12 +379,12 @@
             block = rows(c, ROWS)
             grad = dgbuf[block, :]
             qgc[block, :] = (grad * zbuf[block, :]).astype(BF16)
-            dzb[block, :] = (grad * qc[block, :].astype(F32)).astype(BF16)
+            qc[block, :] = (grad * qc[block, :].astype(F32)).astype(BF16)
             send_back(qgc, qg_out, 0, c)
             return carry
 
         lax.fori_loop(0, 8, step, 0)
-        forward(dzb, spec_d, zz * 2, 2)
+        forward(qc, spec_d, zz * 2, 2)
 
     gather_far(0, True)
     gather_far(1, True)
@@ -409,34 +429,6 @@
     own_qg = keep_back(qgc, qg_out, 0)
     own_qg.start()
     reduce_slab(2)
-    def correlate(re, im, lane, sign):
-        gre = [spec_g[a, re, lane] for a in range(4)]
-        gim = [spec_g[a, im, lane] for a in range(4)]
-        dre = [spec_d[a, re, lane] for a in range(4)]
-        dim = [spec_d[a, im, lane] for a in range(4)]
-        for a in range(4):
-            prod[a, re, lane] = sum(gre[i - a] * dre[i] + gim[i - a] * dim[i] for i in range(a, 4)).astype(BF16)
-            prod[a, im, lane] = sum(gre[i - a] * dim[i] - gim[i - a] * dre[i] for i in range(a, 4)).astype(BF16)
-
-    over_tiles(correlate)
-
-    def grad_prod(i, carry):
-        duc[rows(i, BLOCK), :] = jnp.dot(inv[...], prod[i], preferred_element_type=F32).astype(BF16)
-        return carry
-
-    lax.fori_loop(0, 4, grad_prod, 0)
-
-    def send_grad_prod(off, carry):
-        c = lax.rem(ctx + off, 8)
-        send_back(duc, dul, 1, (1 - zl) * 8 + c)
-        send_back(duc, dul, 1, zl * 8 + c)
-        return carry
-
-    lax.fori_loop(0, 8, send_grad_prod, 0)
-    own_du = keep_back(duc, dul, 1)
-    own_du.start()
-    weight_term(3)
-
     def filter_product(re, im, lane, sign):
         ure = [spec_u[a, re, lane] for a in range(4)]
         uim = [spec_u[a, im, lane] for a in range(4)]
@@ -472,7 +464,33 @@
     lax.fori_loop(1, 4, filter_term, 0)
     fown[...] = filter_of(x)
 
-    reduce_slab(3)
+    def correlate(re, im, lane, sign):
+        gre = [spec_g[a, re, lane] for a in range(4)]
+        gim = [spec_g[a, im, lane] for a in range(4)]
+        dre = [spec_d[a, re, lane] for a in range(4)]
+        dim = [spec_d[a, im, lane] for a in range(4)]
+        for a in range(4):
+            prod[a, re, lane] = sum(gre[i - a] * dre[i] + gim[i - a] * dim[i] for i in range(a, 4)).astype(BF16)
+            prod[a, im, lane] = sum(gre[i - a] * dim[i] - gim[i - a] * dre[i] for i in range(a, 4)).astype(BF16)
+
+    over_tiles(correlate)
+
+    def grad_prod(i, carry):
+        duc[rows(i, BLOCK), :] = jnp.dot(inv[...], prod[i], preferred_element_type=F32).astype(BF16)
+        return carry
+
+    lax.fori_loop(0, 4, grad_prod, 0)
+
+    def send_grad_prod(off, carry):
+        c = lax.rem(ctx + off, 8)
+        send_back(duc, dul, 1, (1 - zl) * 8 + c)
+        send_back(duc, dul, 1, zl * 8 + c)
+        return carry
+
+    lax.fori_loop(0, 8, send_grad_prod, 0)
+    own_du = keep_back(duc, dul, 1)
+    own_du.start()
+    weight_term(3)
     def filter_sum(zz):
         wait_recv(frecv.at[0, pl.ds(0, 3 * ROWS), :], ss_f.at[0], rs_f.at[zz])
         total = fown[rows(zz, ROWS), :]
@@ -484,6 +502,7 @@
         zz = lax.rem(zh + away, 4)
         fsend2[zz] = filter_sum(zz).astype(BF16)
         remote(fsend2.at[zz], frecv2.at[zh], ss_f.at[1], rs_f.at[4], dp_dev(x, zz)).start()
+    reduce_slab(3)
     grad = filter_sum(zh)
 
     own_qg.wait()
@@ -504,7 +523,7 @@
     write_k.start()
     write_v.start()
     wait_recv(wrecv2.at[pl.ds(0, 3)], ss_w2.at[0], rs_w2.at[0])
-    weight = wown[zh]
+    weight = wfin[...]
     for off in range(1, 4):
         weight = weight + wrecv2[lax.rem(zh + off, 4)].astype(F32)
     wg_out[...] = weight * (1.0 / 16.0)
@@ -594,13 +613,13 @@
             vmem((CHAN, SEQ), BF16),
             vmem((SEQ, CHAN), BF16),
             vmem((SEQ, CHAN), BF16),
-            vmem((SEQ, CHAN), BF16),
             vmem((ROWS, WIDTH), BF16),
             vmem((PARTS, 4, CHAN, PIECE), BF16),
             vmem((PARTS, 4, CHAN, PIECE), BF16),
             vmem((PARTS, CHAN, PIECE), F32),
             vmem((PARTS, CHAN, PIECE), BF16),
             vmem((4, CHAN, PIECE), BF16),
+            vmem((CHAN, PIECE), F32),
             vmem((4, BLOCK, CHAN), BF16),
             vmem((4, BLOCK, CHAN), BF16),
             vmem((BLOCK, CHAN), F32),

time: 140 us -> 138 us (0.986)
  Pallas kernels: 139 us -> 137 us
    pallas_call x1, Pallas kernels: 136 us -> 134 us  [shards(): pl.pallas_call(kernel, out_shape=outs, in_specs=[anywhere] * 8, out_specs...]
where the time goes in v4:
time: 138 us; the launch traced here: 137 us
  Pallas kernels  137 us (99%)
    pallas_call x1, Pallas kernels, shards(): pl.pallas_call(kernel, out_shape=outs, in_specs=[anywhere] * 8, out_specs...  134 us
    pallas_call x1, Pallas kernels, shards(): pl.pallas_call(hand_over, out_shape=outs, in_specs=[anywhere] * 5, out_sp...  2.96 us

profile of v4, /device:TPU:1, one launch (start us, length us, event | category | flops | bytes accessed | tf_op | source)
XLA Modules:
  0.0 137.3 jit_solution(18104712088808742770)
XLA Ops:
  0.6 133.7 %hyena_backward.1 = (bf16[128,4096]{1,0:T(8,128)(2,1)}, bf16[128,4096]{1,0:T(8,128)(2,1)}, bf16[128,4096]{1,0:T(8,128)(2,1)}, f32[256,256]{1,0:T(8,128)}, f32[128,256]{1,0:T(8,128)}) custom-call(bf16[128,4096]{1,0:T(8,128)(2,1)} %q_in.1, bf16[128,4096]{1,0:T(8,128)(2,1)} %k_in.1, bf16[128,4096]{1,0:T(8,128)(2,1)} %v_in.1, bf16[128,4096]{1,0:T(8,128)(2,1)} %og_in.1, ...), custom_call_target="tpu_custom_call" | custom-call | flops 16000000000 | bytes 16000000 | tf_op jit(solution)/shard_map/hyena_backward/pallas_call | solution.py:592
  134.4 3.0 %hand_over.1 = (bf16[128,4096]{1,0:T(8,128)(2,1)}, bf16[128,4096]{1,0:T(8,128)(2,1)}, bf16[128,4096]{1,0:T(8,128)(2,1)}, f32[256,256]{1,0:T(8,128)}, f32[128,256]{1,0:T(8,128)}) custom-call(bf16[128,4096]{1,0:T(8,128)(2,1)} %get-tuple-element.10.refs_0_, bf16[128,4096]{1,0:T(8,128)(2,1)} %get-tuple-element.11.refs_1_, ...), custom_call_target="tpu_custom_call" | custom-call | bytes 7000000 | tf_op jit(solution)/shard_map/hand_over/pallas_call | solution.py:644

commit v5 on v4

--- a/solution.py
+++ b/solution.py
@@ -557,7 +557,7 @@
     sources, targets, stage, (load_sem, store_sem) = refs[:5], refs[5:10], refs[10:15], refs[15:]
     loads, stores = [], []
     for i, source in enumerate(sources):
-        parts = 2 if source.shape[1] == WIDTH else 1
+        parts = 4 if source.shape[1] == WIDTH else 1
         count = source.shape[0] // parts
         for part in range(parts):
             piece = pl.ds(part * count, count)
@@ -646,7 +646,7 @@
         out_shape=outs,
         in_specs=[anywhere] * 5,
         out_specs=(anywhere,) * 5,
-        scratch_shapes=[vmem(out.shape, out.dtype) for out in outs] + [dma((8,)), dma((8,))],
+        scratch_shapes=[vmem(out.shape, out.dtype) for out in outs] + [dma((14,)), dma((14,))],
         compiler_params=pltpu.CompilerParams(vmem_limit_bytes=60 * 1024 * 1024),
         cost_estimate=pl.CostEstimate(flops=0, bytes_accessed=7_000_000, transcendentals=0),
         name="hand_over",

time: 138 us -> 138 us (level)
  no operation moved by 1% of the time
where the time goes in v5:
time: 138 us; the launch traced here: 137 us
  Pallas kernels  137 us (99%)
    pallas_call x1, Pallas kernels, shards(): pl.pallas_call(kernel, out_shape=outs, in_specs=[anywhere] * 8, out_specs...  134 us
    pallas_call x1, Pallas kernels, shards(): pl.pallas_call(hand_over, out_shape=outs, in_specs=[anywhere] * 5, out_sp...  3.07 us

profile of v5, /device:TPU:1, one launch (start us, length us, event | category | flops | bytes accessed | tf_op | source)
XLA Modules:
  0.0 137.4 jit_solution(8373958471271218961)
XLA Ops:
  0.6 133.7 %hyena_backward.1 = (bf16[128,4096]{1,0:T(8,128)(2,1)}, bf16[128,4096]{1,0:T(8,128)(2,1)}, bf16[128,4096]{1,0:T(8,128)(2,1)}, f32[256,256]{1,0:T(8,128)}, f32[128,256]{1,0:T(8,128)}) custom-call(bf16[128,4096]{1,0:T(8,128)(2,1)} %q_in.1, bf16[128,4096]{1,0:T(8,128)(2,1)} %k_in.1, bf16[128,4096]{1,0:T(8,128)(2,1)} %v_in.1, bf16[128,4096]{1,0:T(8,128)(2,1)} %og_in.1, ...), custom_call_target="tpu_custom_call" | custom-call | flops 16000000000 | bytes 16000000 | tf_op jit(solution)/shard_map/hyena_backward/pallas_call | solution.py:592
  134.4 3.1 %hand_over.1 = (bf16[128,4096]{1,0:T(8,128)(2,1)}, bf16[128,4096]{1,0:T(8,128)(2,1)}, bf16[128,4096]{1,0:T(8,128)(2,1)}, f32[256,256]{1,0:T(8,128)}, f32[128,256]{1,0:T(8,128)}) custom-call(bf16[128,4096]{1,0:T(8,128)(2,1)} %get-tuple-element.10.refs_0_, bf16[128,4096]{1,0:T(8,128)(2,1)} %get-tuple-element.11.refs_1_, ...), custom_call_target="tpu_custom_call" | custom-call | bytes 7000000 | tf_op jit(solution)/shard_map/hand_over/pallas_call | solution.py:644
